TPU v7x, 256 devices: a whole 4x4x8 slice. The times are simulated.
256 devices in a mesh: rep: 2 (over y_lo), seq: 64 (over x, z, core), chan: 2 (over y_hi).
Axes of the slice: x: 4, y: 4 (y_hi: 2, y_lo: 2; y = y_hi * 2 + y_lo), z: 8, core: 2. Of those that a mesh axis runs over, the one named last changes fastest.
Arguments:
- inputs: bfloat16 [2, 65536, 256], P('rep', 'seq', 'chan'), may hold values from -6 to 6
- cotangent: bfloat16 [2, 65536, 256], P('rep', 'seq', 'chan'), may hold values from -0.015625 to 0.015625
- filter_taps: bfloat16 [65536, 256], P('seq', 'chan'), may hold values from -6 to 6
- out_proj: bfloat16 [256, 256], P('chan'), may hold values from -0.375 to 0.375
Outputs:
- grad_input: bfloat16 [2, 65536, 256], P('rep', 'seq', 'chan')
- grad_filter: float32 [65536, 256], P('seq', 'chan')
All inputs are finite; a program needn't handle non-finite values.
Results may differ from a plain program's by a relative error of at most 0.0049.
Values may be sent and summed in bfloat16 or wider, within the bound.
A program may use at most 128 MiB of HBM per device.

v0:
```python
import math

import jax
import jax.numpy as jnp
from jax import lax
from jax.sharding import PartitionSpec as P

FACTOR = 16


precise_mode = lax.Precision.HIGHEST


def angle_table(numerator, modulus):
    return (numerator % modulus).astype(jnp.float32) * (2.0 * math.pi / modulus)


def dft_table(table_size, direction):
    index_row = jnp.arange(table_size, dtype=jnp.int32)
    angle_grid = angle_table(index_row[:, None] * index_row[None, :], table_size)
    return (jnp.cos(angle_grid), direction * jnp.sin(angle_grid))


def complex_apply(pattern, matrix, real_part, imag_part):
    matrix_real, matrix_imag = matrix

    def product(first_op, second_op):
        return jnp.einsum(pattern, first_op, second_op, precision=precise_mode)

    return (
        product(matrix_real, real_part) - product(matrix_imag, imag_part),
        product(matrix_real, imag_part) + product(matrix_imag, real_part),
    )


def rotate(real_part, imag_part, angle_grid, direction):
    cosine = jnp.cos(angle_grid)
    sine_part = direction * jnp.sin(angle_grid)
    return (real_part * cosine - imag_part * sine_part, real_part * sine_part + imag_part * cosine)


def twist_signal(values, positions, seq_length):
    angle_grid = angle_table(positions, 2 * seq_length)[:, :, None]
    real_part = jnp.stack([values, values * jnp.cos(angle_grid)])
    imag_part = jnp.stack([jnp.zeros_like(values), -values * jnp.sin(angle_grid)])
    return (real_part, imag_part)


def untwist(real_part, imag_part, positions, seq_length):
    angle_grid = angle_table(positions, 2 * seq_length)[:, :, None]
    running = real_part[0] + real_part[1] * jnp.cos(angle_grid) - imag_part[1] * jnp.sin(angle_grid)
    return running / (2.0 * seq_length)


def twiddle_rows(real_part, imag_part, freq_index, row_index, seq_length, direction):
    angle_grid = angle_table(freq_index[:, None] * row_index[None, :], seq_length)[None, :, :, None]
    return rotate(real_part, imag_part, angle_grid, direction)


def rows_forward(real_part, imag_part):
    twists, groups, tok_rows, part_width = real_part.shape
    outer_size = tok_rows // FACTOR
    real_part = real_part.reshape(twists, groups, outer_size, FACTOR, part_width)
    imag_part = imag_part.reshape(twists, groups, outer_size, FACTOR, part_width)
    real_part, imag_part = complex_apply(
        "qr,bkrsc->bkqsc", dft_table(outer_size, -1.0), real_part, imag_part
    )
    outer_index = jnp.arange(outer_size, dtype=jnp.int32)
    inner_index = jnp.arange(FACTOR, dtype=jnp.int32)
    angle_grid = angle_table(outer_index[:, None] * inner_index[None, :], tok_rows)[
        None, None, :, :, None
    ]
    real_part, imag_part = rotate(real_part, imag_part, angle_grid, -1.0)
    return complex_apply("ps,bkqsc->bkqpc", dft_table(FACTOR, -1.0), real_part, imag_part)


def rows_inverse(real_part, imag_part):
    twists, groups, outer_size, inner_size, part_width = real_part.shape
    tok_rows = outer_size * inner_size
    real_part, imag_part = complex_apply(
        "sp,bkqpc->bkqsc", dft_table(inner_size, 1.0), real_part, imag_part
    )
    outer_index = jnp.arange(outer_size, dtype=jnp.int32)
    inner_index = jnp.arange(inner_size, dtype=jnp.int32)
    angle_grid = angle_table(outer_index[:, None] * inner_index[None, :], tok_rows)[
        None, None, :, :, None
    ]
    real_part, imag_part = rotate(real_part, imag_part, angle_grid, 1.0)
    real_part, imag_part = complex_apply(
        "rq,bkqsc->bkrsc", dft_table(outer_size, 1.0), real_part, imag_part
    )
    return (
        real_part.reshape(twists, groups, tok_rows, part_width),
        imag_part.reshape(twists, groups, tok_rows, part_width),
    )


def conj_product(first_real, first_imag, second_real, second_imag):
    return (
        first_real * second_real + first_imag * second_imag,
        first_imag * second_real - first_real * second_imag,
    )


def per_device(inputs, cotangent, filter_taps, out_proj):
    devices = lax.axis_size("seq")
    seq_index = lax.axis_index("seq")
    tok_rows = inputs.shape[1]
    chan_width = inputs.shape[2]
    seq_length = devices * tok_rows
    grad_seq = cotangent.reshape(tok_rows, chan_width)
    projected = lax.dot_general(
        lax.all_gather(grad_seq, "chan", axis=1, tiled=True),
        out_proj,
        (((1,), (1,)), ((), ())),
        preferred_element_type=jnp.float32,
    )
    grad_mixed = projected.astype(jnp.bfloat16)
    signals = (grad_mixed, inputs.reshape(tok_rows, chan_width), filter_taps)
    device_index = jnp.arange(devices, dtype=jnp.int32)
    block_rows = tok_rows // devices
    pieces = (
        lax.all_to_all(signals[0], "seq", split_axis=0, concat_axis=0, tiled=True),
        lax.all_to_all(signals[1], "seq", split_axis=0, concat_axis=0, tiled=True),
        lax.all_to_all(signals[2], "seq", split_axis=0, concat_axis=0, tiled=True),
    )
    stacked = jnp.concatenate([member.astype(jnp.float32) for member in pieces], axis=1)
    stacked = stacked.reshape(devices, block_rows, 3 * chan_width)
    local_rows = seq_index * block_rows + jnp.arange(block_rows, dtype=jnp.int32)
    positions = device_index[:, None] * tok_rows + local_rows[None, :]
    real_part, imag_part = twist_signal(stacked, positions, seq_length)
    real_part, imag_part = complex_apply(
        "kp,bpsc->bksc", dft_table(devices, -1.0), real_part, imag_part
    )
    real_part, imag_part = twiddle_rows(
        real_part, imag_part, device_index, local_rows, seq_length, -1.0
    )
    real_part, imag_part = (
        lax.all_to_all(real_part, "seq", split_axis=1, concat_axis=2, tiled=True),
        lax.all_to_all(imag_part, "seq", split_axis=1, concat_axis=2, tiled=True),
    )
    real_part, imag_part = rows_forward(real_part, imag_part)
    part_width = real_part.shape[-1] // 3
    grad_real = real_part[..., :part_width]
    grad_imag = imag_part[..., :part_width]
    input_real = real_part[..., part_width : 2 * part_width]
    input_imag = imag_part[..., part_width : 2 * part_width]
    taps_real = real_part[..., 2 * part_width :]
    taps_imag = imag_part[..., 2 * part_width :]
    du_real, du_imag = conj_product(grad_real, grad_imag, taps_real, taps_imag)
    dk_real, dk_imag = conj_product(grad_real, grad_imag, input_real, input_imag)
    dk_real, dk_imag = lax.psum((dk_real, dk_imag), "rep")
    joined_real = jnp.concatenate([du_real, dk_real], axis=4)
    joined_imag = jnp.concatenate([du_imag, dk_imag], axis=4)
    real_part, imag_part = rows_inverse(joined_real, joined_imag)
    freq_here = jnp.reshape(seq_index, (1,))
    all_rows = jnp.arange(tok_rows, dtype=jnp.int32)
    real_part, imag_part = twiddle_rows(real_part, imag_part, freq_here, all_rows, seq_length, 1.0)
    real_part, imag_part = (
        lax.all_to_all(real_part, "seq", split_axis=2, concat_axis=1, tiled=True),
        lax.all_to_all(imag_part, "seq", split_axis=2, concat_axis=1, tiled=True),
    )
    real_part, imag_part = complex_apply(
        "pk,bksc->bpsc", dft_table(devices, 1.0), real_part, imag_part
    )
    values = untwist(real_part, imag_part, positions, seq_length)
    grad_rows = values[:, :, :part_width].astype(jnp.bfloat16).reshape(tok_rows, part_width)
    grad_input = lax.all_to_all(grad_rows, "seq", split_axis=0, concat_axis=0, tiled=True)
    filter_rows = values[:, :, part_width:].reshape(tok_rows, values.shape[2] - part_width)
    grad_filter = lax.all_to_all(filter_rows, "seq", split_axis=0, concat_axis=0, tiled=True)
    return (grad_input.reshape(1, tok_rows, chan_width), grad_filter)


def solution(mesh):
    return jax.shard_map(
        per_device,
        mesh=mesh,
        in_specs=(
            P("rep", "seq", "chan"),
            P("rep", "seq", "chan"),
            P("seq", "chan"),
            P("chan", None),
        ),
        out_specs=(P("rep", "seq", "chan"), P("seq", "chan")),
        check_vma=False,
    )
```

profile of v0, /device:TPU:1, one launch (start us, length us, event | category | flops | bytes accessed | tf_op | source)
XLA Modules:
  0.0 586.2 jit_solution(16802311897165362928)
XLA Ops:
  7.2 9.9 %all-gather = bf16[1,1024,256]{2,1,0:T(8,128)(2,1)S(1)} all-gather(bf16[1,1024,128]{2,1,0:T(8,128)(2,1)} %param.5), channel_id=2, replica_groups=mesh['rep'=2,'seq'=64,'chan'=2] {'chan'}, dimensions={2}, use_global_device_ids=true | all-gather | bytes 786432 | tf_op jit(solution)/shard_map/all_gather | solution.py:113
  17.1 0.3 convolution_convert_fusion
  17.4 25.4 %all_to_all.84 = bf16[64,16,128]{2,1,0:T(8,128)(2,1)S(1)} all-to-all(bf16[64,16,128]{2,1,0:T(8,128)(2,1)S(1)} %bitcast.244), channel_id=1, replica_groups=mesh['rep'=2,'seq'=64,'chan'=2] {'seq'}, dimensions={0} | all-to-all | bytes 524288 | tf_op jit(solution)/shard_map/all_to_all | solution.py:123
  42.9 17.8 %all_to_all.85 = bf16[64,16,128]{2,1,0:T(8,128)(2,1)S(1)} all-to-all(bf16[64,16,128]{2,1,0:T(8,128)(2,1)S(1)} %bitcast.245), channel_id=1, replica_groups=mesh['rep'=2,'seq'=64,'chan'=2] {'seq'}, dimensions={0} | all-to-all | bytes 524288 | tf_op jit(solution)/shard_map/all_to_all | solution.py:125
  60.7 6.5 %all-to-all-start.1 = ((bf16[64,16,128]{2,1,0:T(8,128)(2,1)}), bf16[64,16,128]{2,1,0:T(8,128)(2,1)S(1)}, u32[]{:S(2)}, u32[]{:S(2)}) async-start(bf16[64,16,128]{2,1,0:T(8,128)(2,1)} %bitcast.3), calls=%async_computation.1 | async-start | bytes 524288 | tf_op jit(solution)/shard_map/all_to_all | solution.py:124
  67.2 0.2 fusion.182
  67.5 11.5 %all-to-all-done.1 = bf16[64,16,128]{2,1,0:T(8,128)(2,1)S(1)} async-done(((bf16[64,16,128]{2,1,0:T(8,128)(2,1)}), bf16[64,16,128]{2,1,0:T(8,128)(2,1)S(1)}, u32[]{:S(2)}, u32[]{:S(2)}) %all-to-all-start.1) | async-done | bytes 262176 | tf_op jit(solution)/shard_map/all_to_all | solution.py:124
  79.1 0.1 fusion.296
  79.3 2.4 fusion.72
  81.6 2.4 fusion.73
  84.0 0.2 convert_multiply_fusion
  84.2 3.3 fusion.56
  87.5 17.7 %fusion.4 = (f32[2,64,16,384]{3,1,2,0:T(8,128)}, f32[2,64,16,384]{3,1,2,0:T(8,128)S(1)}) fusion(f32[2,16,384,64]{2,3,1,0:T(8,128)S(1)} %fusion.56, f32[64,16]{0,1:T(8,128)S(1)} %get-tuple-element.19, f32[64,16]{0,1:T(8,128)S(1)} %get-tuple-element.18, f32[2,16,384,64]{2,3,1,0:T(8,128)S(1)} %fusion.73, f32[1,64,16,384]{3,1,2,0:T(8,128)S(1)} %convert_multiply_fusion, ...), kind=kOutput, calls=%fused_computation.11 | convolution fusion | flops 610332672 | bytes 15736832 | tf_op jit(solution)/shard_map/kp,bpsc->bksc/dot_general | solution.py:28
  105.3 3.5 copy.43
  108.8 6.0 %all-to-all-start.4 = ((f32[2,64,16,384]{3,2,0,1:T(8,128)}), f32[2,64,16,384]{3,2,0,1:T(8,128)S(1)}, u32[]{:S(2)}, u32[]{:S(2)}) async-start(f32[2,64,16,384]{3,2,0,1:T(8,128)} %copy.43), calls=%async_computation.4 | async-start | bytes 6291456 | tf_op jit(solution)/shard_map/all_to_all | solution.py:140
  114.8 5.3 copy.41
  120.2 68.2 %all-to-all-done.4 = f32[2,64,16,384]{3,2,0,1:T(8,128)S(1)} async-done(((f32[2,64,16,384]{3,2,0,1:T(8,128)}), f32[2,64,16,384]{3,2,0,1:T(8,128)S(1)}, u32[]{:S(2)}, u32[]{:S(2)}) %all-to-all-start.4) | async-done | bytes 3145760 | tf_op jit(solution)/shard_map/all_to_all | solution.py:140
  188.4 1.7 copy-done.2
  190.1 6.1 %all-to-all-start.3 = ((f32[2,64,16,384]{3,2,0,1:T(8,128)}), f32[2,64,16,384]{3,2,0,1:T(8,128)S(1)}, u32[]{:S(2)}, u32[]{:S(2)}) async-start(f32[2,64,16,384]{3,2,0,1:T(8,128)} %copy.41), calls=%async_computation.3 | async-start | bytes 6291456 | tf_op jit(solution)/shard_map/all_to_all | solution.py:139
  196.3 8.5 %fusion.16 = f32[2,16,384,64]{2,3,1,0:T(8,128)} fusion(f32[2,64,16,384]{3,2,0,1:T(8,128)} %copy-done.2), kind=kOutput, calls=%fused_computation.27 | convolution fusion | flops 604041216 | bytes 6291456 | tf_op jit(solution)/shard_map/qr,bkrsc->bkqsc/dot_general | solution.py:28
  204.8 6.6 %fusion.14 = f32[2,16,384,64]{2,3,1,0:T(8,128)} fusion(f32[2,64,16,384]{3,2,0,1:T(8,128)S(1)} %copy-done.3), kind=kOutput, calls=%fused_computation.25 | convolution fusion | flops 604037120 | bytes 6291456 | tf_op jit(solution)/shard_map/qr,bkrsc->bkqsc/dot_general | solution.py:28
  211.4 58.2 %all-to-all-done.3 = f32[2,64,16,384]{3,2,0,1:T(8,128)S(1)} async-done(((f32[2,64,16,384]{3,2,0,1:T(8,128)}), f32[2,64,16,384]{3,2,0,1:T(8,128)S(1)}, u32[]{:S(2)}, u32[]{:S(2)}) %all-to-all-start.3) | async-done | bytes 3145760 | tf_op jit(solution)/shard_map/all_to_all | solution.py:139
  269.7 7.5 %fusion.46 = f32[2,16,384,64]{2,3,1,0:T(8,128)S(1)} fusion(f32[2,16,384,64]{2,3,1,0:T(8,128)} %fusion.16, f32[2,64,16,384]{3,2,0,1:T(8,128)S(1)} %all-to-all-done.3), kind=kOutput, calls=%fused_computation.71 | convolution fusion | flops 604823552 | bytes 9437184 | tf_op jit(solution)/shard_map/qr,bkrsc->bkqsc/dot_general | solution.py:28
  277.2 6.2 %fusion.1 = (f32[2,64,16,384]{3,1,2,0:T(8,128)S(1)}, f32[2,64,16,384]{3,1,2,0:T(8,128)S(1)}) fusion(f32[2,16,384,64]{2,3,1,0:T(8,128)S(1)} %fusion.46, f32[64,16]{0,1:T(8,128)S(1)} %get-tuple-element.24, f32[64,16]{0,1:T(8,128)S(1)} %get-tuple-element.25, f32[2,16,384,64]{2,3,1,0:T(8,128)S(1)} %copy-done.4, f32[2,64,16,384]{3,2,0,1:T(8,128)S(1)} %all-to-all-done.3), kind=kOutput, calls=%fused_computation.4 | convolution fusion | flops 609546240 | bytes 15736832 | tf_op jit(solution)/shard_map/qr,bkrsc->bkqsc/dot_general | solution.py:28
  283.4 4.8 fusion.8
  288.3 4.7 fusion.6
  293.0 4.8 subtract_bitcast_fusion
  297.8 5.0 add_bitcast_fusion
  302.8 1.8 multiply_add_fusion.1
  304.6 0.1 copy.51
  304.9 71.6 %all-reduce.4.cloned.1.call-done = (f32[2,1,64,16,128]{4,3,2,0,1:T(8,128)}, f32[2,1,64,16,128]{4,3,2,0,1:T(8,128)}) async-done(((f32[2,1,64,16,128]{4,3,2,0,1:T(8,128)}, f32[2,1,64,16,128]{4,3,2,0,1:T(8,128)}), (f32[2,1,64,16,128]{4,3,2,0,1:T(8,128)}, f32[2,1,64,16,128]{4,3,2,0,1:T(8,128)})) %all-reduce.4.cloned.1.call-update) | async-done | bytes 2097168 | tf_op jit(solution)/shard_map/psum | solution.py:152
  376.5 3.3 fusion.58
  379.8 2.0 fusion.59
  381.8 2.1 fusion.62
  383.9 3.0 fusion.27
  387.0 3.4 fusion.40
  390.4 3.3 fusion.38
  393.7 3.5 subtract_bitcast_fusion.2
  397.2 1.2 copy.55
  398.4 3.6 add_bitcast_fusion.2
  402.0 1.2 copy.58
  403.2 0.5 fusion.24
  403.7 2.9 copy.62
  406.7 10.9 %all-to-all-start.6 = ((f32[2,1,1024,256]{3,0,1,2:T(2,128)}), f32[2,1,1024,256]{3,0,1,2:T(2,128)}, u32[]{:S(2)}, u32[]{:S(2)}) async-start(f32[2,1,1024,256]{3,0,1,2:T(2,128)} %copy.62), calls=%async_computation.6 | async-start | bytes 4194304 | tf_op jit(solution)/shard_map/all_to_all | solution.py:161
  417.5 3.0 copy.59
  420.5 48.2 %all-to-all-done.6 = f32[2,1,1024,256]{3,0,1,2:T(2,128)} async-done(((f32[2,1,1024,256]{3,0,1,2:T(2,128)}), f32[2,1,1024,256]{3,0,1,2:T(2,128)}, u32[]{:S(2)}, u32[]{:S(2)}) %all-to-all-start.6) | async-done | bytes 2097184 | tf_op jit(solution)/shard_map/all_to_all | solution.py:161
  468.7 6.2 %all-to-all-start.5 = ((f32[2,1,1024,256]{3,0,1,2:T(2,128)}), f32[2,1,1024,256]{3,0,1,2:T(2,128)}, u32[]{:S(2)}, u32[]{:S(2)}) async-start(f32[2,1,1024,256]{3,0,1,2:T(2,128)} %copy.59), calls=%async_computation.5 | async-start | bytes 4194304 | tf_op jit(solution)/shard_map/all_to_all | solution.py:160
  474.9 1.8 copy.63
  476.7 4.7 fusion.32
  481.4 3.3 fusion.30
  484.7 41.2 %all-to-all-done.5 = f32[2,1,1024,256]{3,0,1,2:T(2,128)} async-done(((f32[2,1,1024,256]{3,0,1,2:T(2,128)}), f32[2,1,1024,256]{3,0,1,2:T(2,128)}, u32[]{:S(2)}, u32[]{:S(2)}) %all-to-all-start.5) | async-done | bytes 2097184 | tf_op jit(solution)/shard_map/all_to_all | solution.py:160
  525.9 1.9 copy.60
  527.8 0.3 copy-done.5
  528.1 3.3 subtract_bitcast_fusion.1
  531.4 3.6 add_bitcast_fusion.1
  535.1 0.4 fusion.78
  535.5 0.9 copy.67
  536.4 5.8 all-to-all-start.7
  542.2 1.1 copy.68
  543.3 10.8 %all-to-all-done.7 = bf16[64,16,128]{2,1,0:T(8,128)(2,1)S(1)} async-done(((bf16[64,16,128]{2,1,0:T(8,128)(2,1)}), bf16[64,16,128]{2,1,0:T(8,128)(2,1)S(1)}, u32[]{:S(2)}, u32[]{:S(2)}) %all-to-all-start.7) | async-done | bytes 262176 | tf_op jit(solution)/shard_map/all_to_all | solution.py:168
  554.2 6.0 %all-to-all-start.8 = ((f32[64,16,128]{2,1,0:T(8,128)}), f32[64,16,128]{2,1,0:T(8,128)S(1)}, u32[]{:S(2)}, u32[]{:S(2)}) async-start(f32[64,16,128]{2,1,0:T(8,128)} %copy.68), calls=%async_computation.8 | async-start | bytes 1048576 | tf_op jit(solution)/shard_map/all_to_all | solution.py:170
  560.2 17.3 %all-to-all-done.8 = f32[64,16,128]{2,1,0:T(8,128)S(1)} async-done(((f32[64,16,128]{2,1,0:T(8,128)}), f32[64,16,128]{2,1,0:T(8,128)S(1)}, u32[]{:S(2)}, u32[]{:S(2)}) %all-to-all-start.8) | async-done | bytes 524320 | tf_op jit(solution)/shard_map/all_to_all | solution.py:170
  577.5 0.7 copy.135
  578.3 0.8 copy.136
  (29 shorter events, 0.6 us)
Async XLA Ops:
  7.2 10.0 %copy-start = (bf16[128,256]{1,0:T(8,128)(2,1)S(1)}, bf16[128,256]{1,0:T(8,128)(2,1)}, u32[]{:S(2)}) copy-start(bf16[128,256]{1,0:T(8,128)(2,1)} %param.7) | copy-start | bytes 196612
  7.2 35.7 %copy-start.8 = (bf16[1024,128]{1,0:T(8,128)(2,1)S(1)}, bf16[1024,128]{1,0:T(8,128)(2,1)}, u32[]{:S(2)}) copy-start(bf16[1024,128]{1,0:T(8,128)(2,1)} %param.6) | copy-start | bytes 786436
  60.7 18.4 %all-to-all-start.1 = ((bf16[64,16,128]{2,1,0:T(8,128)(2,1)}), bf16[64,16,128]{2,1,0:T(8,128)(2,1)S(1)}, u32[]{:S(2)}, u32[]{:S(2)}) async-start(bf16[64,16,128]{2,1,0:T(8,128)(2,1)} %bitcast.3), calls=%async_computation.1 | async-start | bytes 524288 | tf_op jit(solution)/shard_map/all_to_all | solution.py:124
  108.8 79.5 %all-to-all-start.4 = ((f32[2,64,16,384]{3,2,0,1:T(8,128)}), f32[2,64,16,384]{3,2,0,1:T(8,128)S(1)}, u32[]{:S(2)}, u32[]{:S(2)}) async-start(f32[2,64,16,384]{3,2,0,1:T(8,128)} %copy.43), calls=%async_computation.4 | async-start | bytes 6291456 | tf_op jit(solution)/shard_map/all_to_all | solution.py:140
  188.3 1.7 copy-start.2
  190.1 79.6 %all-to-all-start.3 = ((f32[2,64,16,384]{3,2,0,1:T(8,128)}), f32[2,64,16,384]{3,2,0,1:T(8,128)S(1)}, u32[]{:S(2)}, u32[]{:S(2)}) async-start(f32[2,64,16,384]{3,2,0,1:T(8,128)} %copy.41), calls=%async_computation.3 | async-start | bytes 6291456 | tf_op jit(solution)/shard_map/all_to_all | solution.py:139
  196.2 180.4 %all-reduce.4.cloned.1.call-start = ((), (), s32[]{:S(2)}) async-start(), calls=%async_computation.9 | async-start | bytes 4194304 | tf_op jit(solution)/shard_map/psum | solution.py:152
  196.3 8.5 %copy-start.3 = (f32[2,64,16,384]{3,2,0,1:T(8,128)S(1)}, f32[2,64,16,384]{3,2,0,1:T(8,128)}, u32[]{:S(2)}) copy-start(f32[2,64,16,384]{3,2,0,1:T(8,128)} %copy-done.2) | copy-start | bytes 9437188
  269.7 7.5 %copy-start.4 = (f32[2,16,384,64]{2,3,1,0:T(8,128)S(1)}, f32[2,16,384,64]{2,3,1,0:T(8,128)}, u32[]{:S(2)}) copy-start(f32[2,16,384,64]{2,3,1,0:T(8,128)} %fusion.14) | copy-start | bytes 9437188
  376.5 3.3 copy-start.7
  379.8 2.0 copy-start.6
  406.7 62.0 %all-to-all-start.6 = ((f32[2,1,1024,256]{3,0,1,2:T(2,128)}), f32[2,1,1024,256]{3,0,1,2:T(2,128)}, u32[]{:S(2)}, u32[]{:S(2)}) async-start(f32[2,1,1024,256]{3,0,1,2:T(2,128)} %copy.62), calls=%async_computation.6 | async-start | bytes 4194304 | tf_op jit(solution)/shard_map/all_to_all | solution.py:161
  468.7 57.2 %all-to-all-start.5 = ((f32[2,1,1024,256]{3,0,1,2:T(2,128)}), f32[2,1,1024,256]{3,0,1,2:T(2,128)}, u32[]{:S(2)}, u32[]{:S(2)}) async-start(f32[2,1,1024,256]{3,0,1,2:T(2,128)} %copy.59), calls=%async_computation.5 | async-start | bytes 4194304 | tf_op jit(solution)/shard_map/all_to_all | solution.py:160
  525.9 2.2 copy-start.5
  536.4 17.8 %all-to-all-start.7 = ((bf16[64,16,128]{2,1,0:T(8,128)(2,1)}), bf16[64,16,128]{2,1,0:T(8,128)(2,1)S(1)}, u32[]{:S(2)}, u32[]{:S(2)}) async-start(bf16[64,16,128]{2,1,0:T(8,128)(2,1)} %copy.67), calls=%async_computation.7 | async-start | bytes 524288 | tf_op jit(solution)/shard_map/all_to_all | solution.py:168
  542.2 36.9 %copy-start.1 = (bf16[128,256]{1,0:T(8,128)(2,1)S(1)}, bf16[128,256]{1,0:T(8,128)(2,1)}, u32[]{:S(2)}) copy-start(bf16[128,256]{1,0:T(8,128)(2,1)} %param.7) | copy-start | bytes 196612
  554.2 23.4 %all-to-all-start.8 = ((f32[64,16,128]{2,1,0:T(8,128)}), f32[64,16,128]{2,1,0:T(8,128)S(1)}, u32[]{:S(2)}, u32[]{:S(2)}) async-start(f32[64,16,128]{2,1,0:T(8,128)} %copy.68), calls=%async_computation.8 | async-start | bytes 1048576 | tf_op jit(solution)/shard_map/all_to_all | solution.py:170
Sparse Core Ops, SparseCore 0:
  304.7 71.7 all-reduce.3
where the time goes:
time: 590 us; the launch traced here: 586 us
  waiting for transfers between devices  327 us (55%)
  matrix products  113 us (19%)
  blocking collectives  53.2 us (9%)
  starting transfers between devices  47.6 us (8%)
  local copies, waits for them, and re-layouts  26.9 us (5%)
  between operations  14.7 us (2%)
    dot_general x24, matrix products, product(): return jnp.einsum(pattern, first_op, second_op, precision=precise_mode)  113 us
    psum x1, waiting for transfers between devices, per_device(): dk_real, dk_imag = lax.psum((dk_real, dk_imag), 'rep')  71.6 us
    all_to_all x1, waiting for transfers between devices, per_device(): lax.all_to_all(imag_part, 'seq', split_axis=1, concat_axis=2, tiled=True)  68.2 us
    all_to_all x1, waiting for transfers between devices, per_device(): lax.all_to_all(real_part, 'seq', split_axis=1, concat_axis=2, tiled=True)  58.2 us
    all_to_all x1, waiting for transfers between devices, per_device(): lax.all_to_all(imag_part, 'seq', split_axis=2, concat_axis=1, tiled=True)  48.2 us
    all_to_all x1, waiting for transfers between devices, per_device(): lax.all_to_all(real_part, 'seq', split_axis=2, concat_axis=1, tiled=True)  41.2 us
    all_to_all x1, blocking collectives, per_device(): lax.all_to_all(signals[0], 'seq', split_axis=0, concat_axis=0, tiled=True)  25.4 us
    all_to_all x1, blocking collectives, per_device(): lax.all_to_all(signals[2], 'seq', split_axis=0, concat_axis=0, tiled=True)  17.8 us
  transfers between devices with their start and end apart: 8, of which 8 were waited for; matrix products, arithmetic and copies ran while one was open for 6% of the time, Pallas kernels for 0%

commit v1 on v0

v1 whole, which is shorter than its diff:
```python
import math

import jax
import jax.numpy as jnp
import numpy as np
from jax import lax
from jax.sharding import PartitionSpec as P

precise_mode = lax.Precision.HIGHEST
LANES = 128


def tables(length):
    rows = length // LANES
    row_index = np.arange(rows)
    lane_index = np.arange(LANES)
    row_angle = ((4 * row_index[:, None] + 1) * row_index[None, :] % (4 * rows)) * (2.0 * math.pi / (4 * rows))
    twist_angle = ((4 * row_index[:, None] + 1) * lane_index[None, :] % (4 * length)) * (2.0 * math.pi / (4 * length))
    lane_angle = (lane_index[:, None] * lane_index[None, :] % LANES) * (2.0 * math.pi / LANES)
    row_forward = np.concatenate([np.cos(row_angle), -np.sin(row_angle)], axis=0)
    row_inverse = np.concatenate([np.cos(row_angle).T, -np.sin(row_angle).T], axis=1) / length
    lane_cos, lane_sin = np.cos(lane_angle), np.sin(lane_angle)
    lane_forward = np.block([[lane_cos, -lane_sin], [lane_sin, lane_cos]])
    lane_inverse = np.block([[lane_cos, lane_sin], [-lane_sin, lane_cos]])
    return [
        np.asarray(table, np.float32)
        for table in (row_forward, row_inverse, lane_forward, lane_inverse, np.cos(twist_angle), np.sin(twist_angle))
    ]


def product(left, right):
    return jnp.dot(left, right, precision=precise_mode, preferred_element_type=jnp.float32)


def correlate(grads, signals, taps):
    length = taps.shape[0]
    rows = length // LANES
    row_forward, row_inverse, lane_forward, lane_inverse, twist_cos, twist_sin = tables(length)
    stacked = jnp.concatenate([grads, signals, taps[None]], axis=0).astype(jnp.float32)
    count = stacked.shape[0]
    stacked = stacked.reshape(count, rows, LANES).transpose(1, 0, 2).reshape(rows, count * LANES)
    outer = product(row_forward, stacked).reshape(2, rows, count, LANES)
    cosine, sine = twist_cos[:, None, :], twist_sin[:, None, :]
    twisted = jnp.concatenate(
        [outer[0] * cosine + outer[1] * sine, outer[1] * cosine - outer[0] * sine], axis=-1
    )
    spectra = product(twisted.transpose(1, 0, 2).reshape(count * rows, 2 * LANES), lane_forward)
    spectra = spectra.reshape(count, rows, 2, LANES)
    real, imag = spectra[:, :, 0], spectra[:, :, 1]

    def conj_product(first, second):
        return jnp.concatenate(
            [
                real[first] * real[second] + imag[first] * imag[second],
                imag[first] * real[second] - real[first] * imag[second],
            ],
            axis=-1,
        )

    joined = jnp.concatenate(
        [conj_product(0, 4), conj_product(1, 4), conj_product(0, 2) + conj_product(1, 3)], axis=0
    )
    inner = product(joined, lane_inverse).reshape(3, rows, 2, LANES)
    real, imag = inner[:, :, 0], inner[:, :, 1]
    untwisted = jnp.stack(
        [real * twist_cos - imag * twist_sin, imag * twist_cos + real * twist_sin]
    )
    untwisted = untwisted.transpose(0, 2, 1, 3).reshape(2 * rows, 3 * LANES)
    result = product(row_inverse, untwisted)
    return result.reshape(rows, 3, LANES).transpose(1, 0, 2).reshape(3, length)


def per_device(inputs, cotangent, filter_taps, out_proj):
    devices = lax.axis_size("seq")
    members = lax.axis_size("rep")
    member = lax.axis_index("rep")
    tok_rows, chan_width = filter_taps.shape
    gathered = lax.all_gather(cotangent.reshape(tok_rows, chan_width), "chan", axis=1, tiled=True)
    grad_mixed = lax.dot_general(
        out_proj, gathered, (((1,), (1,)), ((), ())), preferred_element_type=jnp.float32
    ).astype(jnp.bfloat16)
    signal = inputs.reshape(tok_rows, chan_width).T
    half = tok_rows // members
    taps = lax.dynamic_slice_in_dim(filter_taps, member * half, half, axis=0).T
    outgoing = jnp.concatenate([grad_mixed, signal, taps], axis=1)
    arrived = lax.all_to_all(outgoing, ("rep", "seq"), split_axis=0, concat_axis=0, tiled=True)
    arrived = arrived.reshape(members, devices, 2 * tok_rows + half)
    grads = arrived[:, :, :tok_rows].reshape(members, devices * tok_rows)
    signals = arrived[:, :, tok_rows : 2 * tok_rows].reshape(members, devices * tok_rows)
    taps = arrived[:, :, 2 * tok_rows :].transpose(1, 0, 2).reshape(devices * tok_rows)
    result = correlate(grads, signals, taps).astype(jnp.bfloat16)
    result = result.reshape(3, devices, tok_rows)
    outgoing = jnp.stack([result[:2], jnp.broadcast_to(result[2:], (2, devices, tok_rows))], axis=2)
    outgoing = outgoing.reshape(members * devices, 2 * tok_rows)
    arrived = lax.all_to_all(outgoing, ("rep", "seq"), split_axis=0, concat_axis=0, tiled=True)
    grad_input = arrived[:, :tok_rows].T
    grad_filter = arrived[:, tok_rows:].T.astype(jnp.float32)
    return (grad_input.reshape(1, tok_rows, chan_width), grad_filter)


def solution(mesh):
    return jax.shard_map(
        per_device,
        mesh=mesh,
        in_specs=(
            P("rep", "seq", "chan"),
            P("rep", "seq", "chan"),
            P("seq", "chan"),
            P("chan", None),
        ),
        out_specs=(P("rep", "seq", "chan"), P("seq", "chan")),
        check_vma=False,
    )
```

time: 590 us -> 114 us (0.19)
  waiting for transfers between devices: 327 us -> 0 us
  matrix products: 113 us -> 12.2 us
  starting transfers between devices: 47.6 us -> 0 us
  blocking collectives: 53.2 us -> 71.4 us
  between operations: 14.7 us -> 1.05 us
  local copies, waits for them, and re-layouts: 26.9 us -> 18.7 us
  other arithmetic: 3.32 us -> 10 us
    all_to_all x7 -> x0, waiting for transfers between devices: 255 us -> none  [the longest x1 68.2 us: per_device(): lax.all_to_all(imag_part, 'seq', split_axis=1, concat_axis=2, tiled=True)]
    dot_general x25 -> x5, matrix products: 113 us -> 12.2 us  [the longest x4 11.9 us: product(): jnp.dot(left, right, precision=precise_mode, preferred_element_type=jnp.f...]
    psum x1 -> x0, waiting for transfers between devices: 71.6 us -> none  [per_device(): dk_real, dk_imag = lax.psum((dk_real, dk_imag), 'rep')]
    all_to_all x7 -> x0, starting transfers between devices: 47.6 us -> none  [the longest x1 10.9 us: per_device(): lax.all_to_all(imag_part, 'seq', split_axis=2, concat_axis=1, tiled=True)]
    all_to_all x2, blocking collectives: 43.2 us -> 61.6 us  [per_device(): lax.all_to_all(outgoing, ('rep', 'seq'), split_axis=0, concat_axis=0, til...]
    sub x3 -> x0, local copies, waits for them, and re-layouts: 9.54 us -> none  [the longest x2 8.32 us: rotate(): real_part * cosine - imag_part * sine_part]
    add x3 -> x0, local copies, waits for them, and re-layouts: 7.7 us -> none  [the longest x2 6.48 us: rotate(): real_part * sine_part + imag_part * cosine]
    unnamed x20 -> x33, local copies, waits for them, and re-layouts: 3.56 us -> 10.8 us
  transfers between devices with their start and end apart: 8 -> 0, of which waited for: 8 -> 0; matrix products, arithmetic and copies ran while one was open for 6% -> 0% of each run, Pallas kernels for 0% -> 0%
where the time goes in v1:
time: 114 us; the launch traced here: 113 us
  blocking collectives  71.4 us (63%)
  local copies, waits for them, and re-layouts  18.7 us (16%)
  matrix products  12.2 us (11%)
  other arithmetic  10 us (9%)
    all_to_all x2, blocking collectives, per_device(): lax.all_to_all(outgoing, ('rep', 'seq'), split_axis=0, concat_axis=0, til...  61.6 us
    dot_general x4, matrix products, product(): jnp.dot(left, right, precision=precise_mode, preferred_element_type=jnp.f...  11.9 us
    unnamed x33, local copies, waits for them, and re-layouts  10.8 us
    all_gather x1, blocking collectives, per_device(): lax.all_gather(cotangent.reshape(tok_rows, chan_width), 'chan', axis=1, t...  9.8 us
    all_to_all x3, other arithmetic, per_device(): lax.all_to_all(outgoing, ('rep', 'seq'), split_axis=0, concat_axis=0, til...  4.85 us

profile of v1, /device:TPU:1, one launch (start us, length us, event | category | flops | bytes accessed | tf_op | source)
XLA Modules:
  0.0 113.5 jit_solution(13418958070580187911)
XLA Ops:
  0.6 0.0 copy-start
  0.6 0.0 copy-start.8
  0.7 0.9 copy-done
  1.6 0.1 copy.92
  1.7 1.1 copy.71
  2.8 9.8 %all-gather = bf16[1,1024,256]{2,1,0:T(8,128)(2,1)S(1)} all-gather(bf16[1,1024,128]{2,1,0:T(8,128)(2,1)} %param.13), channel_id=2, replica_groups=mesh['rep'=2,'seq'=64,'chan'=2] {'chan'}, dimensions={2}, use_global_device_ids=true | all-gather | bytes 786432 | tf_op jit(solution)/shard_map/all_gather | solution.py:78
  12.6 0.0 copy-done.8
  12.6 0.3 convolution_convert_fusion.1
  13.0 0.5 broadcast.31
  13.5 1.1 reduce
  14.6 0.1 reshape.170
  14.8 36.4 %all_to_all.22 = bf16[128,2,1280]{2,1,0:T(2,128)(2,1)S(1)} all-to-all(bf16[128,2,1280]{2,1,0:T(2,128)(2,1)S(1)} %reshape.170), channel_id=1, replica_groups=mesh['rep'=2,'seq'=64,'chan'=2] {'rep','seq'}, dimensions={0} | all-to-all | bytes 1310720 | tf_op jit(solution)/shard_map/all_to_all | solution.py:86
  51.2 0.5 reshape.171
  51.7 0.1 copy.90
  51.8 0.1 fusion.20
  51.9 0.1 concatenate.32
  52.0 0.1 copy.74
  52.2 0.1 concatenate.34
  52.3 0.1 concatenate.33
  52.4 0.1 maximum_bitcast_fusion.3
  52.5 0.2 copy.75
  52.7 3.9 %fusion.21 = f32[1024,640]{0,1:T(8,128)S(1)} fusion(f32[1024,512]{1,0:T(8,128)} %constant.28.clone, bf16[512,640]{0,1:T(8,128)(2,1)S(1)} %bitcast.87), kind=kOutput, calls=%fused_computation.48 | convolution fusion | flops 4026531840 | bytes 5373952 | tf_op jit(solution)/shard_map/dot_general | solution.py:32
  56.6 0.2 fusion.18
  56.9 1.5 %copy.77 = f32[512,5,128]{2,0,1:T(8,128)} copy(f32[512,5,128]{0,2,1:T(8,128)S(1)} %bitcast.84) | data formatting | bytes 2621440 | tf_op jit(solution)/shard_map/squeeze | solution.py:45
  58.4 1.5 %copy.76 = f32[512,5,128]{2,0,1:T(8,128)} copy(f32[512,5,128]{0,2,1:T(8,128)S(1)} %bitcast.83) | data formatting | bytes 2621440 | tf_op jit(solution)/shard_map/squeeze | solution.py:45
  59.8 0.0 copy-done.1
  59.8 0.0 copy-done.5
  59.9 0.3 copy-done.6
  60.1 1.7 %multiply_add_fusion = (f32[512,5,128]{2,0,1:T(8,128)S(1)}, f32[512,5,128]{2,0,1:T(8,128)S(1)}) fusion(f32[512,5,128]{2,0,1:T(8,128)S(1)} %copy-done.1, f32[512,5,128]{2,0,1:T(8,128)} %copy.76, f32[512,128]{1,0:T(8,128)S(1)} %copy-done.5, f32[512,128]{1,0:T(8,128)S(1)} %copy-done.6), kind=kLoop, calls=%fused_computation.16 | loop fusion | flops 1966080 | bytes 5767168 | tf_op jit(solution)/shard_map/add | solution.py:45
  61.8 0.0 copy-done.7
  61.8 2.6 %fusion = f32[5,512,2,128]{1,3,2,0:T(8,128)S(1)} fusion(f32[2,128,256,1]{2,1,0,3:T(8,128)S(1)} %copy-done.7, f32[512,5,128]{2,0,1:T(8,128)S(1)} %get-tuple-element.11, f32[512,5,128]{2,0,1:T(8,128)S(1)} %get-tuple-element.10), kind=kOutput, calls=%fused_computation.1 | convolution fusion | flops 2013921280 | bytes 5505024 | tf_op jit(solution)/shard_map/dot_general | solution.py:32
  64.4 0.2 add_bitcast_fusion.3
  64.6 0.2 subtract_bitcast_fusion.3
  64.8 0.0 copy-start.9
  64.9 0.1 maximum_add_fusion
  64.9 0.9 copy-done.9
  65.8 2.7 %fusion.3 = f32[1536,256]{1,0:T(8,128)S(1)} fusion(f32[256,256]{1,0:T(8,128)S(1)} %copy-done.9, f32[512,256]{0,1:T(8,128)S(1)} %maximum_add_fusion, f32[512,128]{0,1:T(8,128)S(1)} %get-tuple-element.17, f32[512,128]{0,1:T(8,128)S(1)} %get-tuple-element.15, f32[512,128]{0,1:T(8,128)S(1)} %get-tuple-element.16, f32[512,128]{0,1:T(8,128)S(1)} %get-tuple-element.12), kind=kOutput, calls=%fused_computation.4 | convolution fusion | flops 1209532416 | bytes 3407872 | tf_op jit(solution)/shard_map/dot_general | solution.py:32
  68.5 0.8 reshape.164
  69.4 1.2 %fusion.19 = (f32[3,512,1,128]{3,2,1,0:T(1,128)S(1)}, f32[3,512,1,128]{3,2,1,0:T(1,128)S(1)}) fusion(f32[3,512,2,128]{3,2,1,0:T(2,128)S(1)} %reshape.164), kind=kLoop, calls=%fused_computation.46 | loop fusion | bytes 3145728 | tf_op jit(solution)/shard_map/slice | solution.py:64
  70.6 1.2 %copy.93 = f32[3,512,1,128]{1,2,3,0:T(1,128)S(1)} copy(f32[3,512,1,128]{3,2,1,0:T(1,128)S(1)} %get-tuple-element.24) | data formatting | bytes 1572864
  71.8 0.0 copy-start.3
  71.8 0.0 copy-start.4
  71.8 1.0 copy.94
  72.8 0.0 copy-done.4
  72.8 1.4 %fusion.13 = (f32[1,3,512,128]{2,0,3,1:T(1,128)S(1)}, f32[1,3,512,128]{2,0,3,1:T(1,128)S(1)}) fusion(f32[3,512,1,128]{1,2,3,0:T(1,128)S(1)} %copy.94, f32[3,512,1,128]{1,2,3,0:T(1,128)S(1)} %copy.93, f32[512,128]{0,1:T(8,128)S(1)} %copy-done.3, f32[512,128]{0,1:T(8,128)S(1)} %copy-done.4), kind=kLoop, calls=%fused_computation.21 | loop fusion | flops 1179648 | bytes 3670016 | tf_op jit(solution)/shard_map/sub | solution.py:66
  74.2 1.4 %pad_maximum_fusion = f32[2,3,512,128]{2,0,3,1:T(2,128)S(1)} fusion(f32[1,3,512,128]{2,0,3,1:T(1,128)S(1)} %get-tuple-element.23, f32[1,3,512,128]{2,0,3,1:T(1,128)S(1)} %get-tuple-element.22), kind=kLoop, calls=%fused_computation.14 | loop fusion | flops 393216 | bytes 3145728 | tf_op jit(solution)/shard_map/stack | solution.py:65
  75.6 0.0 copy-start.2
  75.6 0.3 copy.95
  76.0 1.2 %copy-done.2 = f32[512,1024]{1,0:T(8,128)S(1)} copy-done((f32[512,1024]{1,0:T(8,128)S(1)}, f32[512,1024]{1,0:T(8,128)}, u32[]{:S(2)}) %copy-start.2) | copy-done | bytes 2097176
  77.2 2.7 %convolution_convert_fusion = bf16[384,512]{1,0:T(8,128)(2,1)S(1)} fusion(f32[1024,384]{0,1:T(8,128)S(1)} %bitcast.82, f32[512,1024]{1,0:T(8,128)S(1)} %copy-done.2), kind=kOutput, calls=%fused_computation.17 | convolution fusion | flops 2416115712 | bytes 4063232 | tf_op jit(solution)/shard_map/dot_general | solution.py:32
  79.9 0.2 copy.84
  80.2 0.1 stack.12
  80.3 0.1 stack_broadcast_in_dim.7
  80.4 0.1 pad_maximum_fusion.1
  80.5 0.5 copy.85
  81.0 0.5 all_to_all.19
  81.5 3.7 %reduce.1 = bf16[128,2048]{1,0:T(8,128)(2,1)S(1)} reduce(bf16[128,1,2048]{2,1,0:T(2,128)(2,1)S(1)} %all_to_all.19, bf16[]{:T(256)} %broadcast.31), dimensions={1}, to_apply=%all_to_all.19.reduce_sub_computation | reduce | bytes 1048578 | tf_op jit(solution)/shard_map/all_to_all | solution.py:95
  85.2 0.4 reshape.172
  85.6 25.2 %all_to_all.23 = bf16[128,2,1024]{2,1,0:T(2,128)(2,1)S(1)} all-to-all(bf16[128,2,1024]{2,1,0:T(2,128)(2,1)S(1)} %reshape.172), channel_id=1, replica_groups=mesh['rep'=2,'seq'=64,'chan'=2] {'rep','seq'}, dimensions={0} | all-to-all | bytes 1048576 | tf_op jit(solution)/shard_map/all_to_all | solution.py:95
  110.8 0.4 reshape.173
  111.2 0.3 copy.97
  111.5 0.1 convert_bitcast_fusion
  111.6 1.0 copy.88
  112.6 0.8 copy.87
  (11 shorter events, 0.1 us)
Async XLA Ops:
  0.6 1.0 copy-start
  0.6 12.0 %copy-start.8 = (bf16[128,256]{1,0:T(8,128)(2,1)S(1)}, bf16[128,256]{1,0:T(8,128)(2,1)}, u32[]{:S(2)}) copy-start(bf16[128,256]{1,0:T(8,128)(2,1)} %param.15) | copy-start | bytes 196612
  58.4 1.5 %copy-start.1 = (f32[512,5,128]{2,0,1:T(8,128)S(1)}, f32[512,5,128]{2,0,1:T(8,128)}, u32[]{:S(2)}) copy-start(f32[512,5,128]{2,0,1:T(8,128)} %copy.77) | copy-start | bytes 3932164
  58.4 1.5 %copy-start.5 = (f32[512,128]{1,0:T(8,128)S(1)}, f32[512,128]{1,0:T(8,128)}, u32[]{:S(2)}) copy-start(f32[512,128]{1,0:T(8,128)} %constant.34.clone) | copy-start | bytes 786436
  58.4 1.7 %copy-start.6 = (f32[512,128]{1,0:T(8,128)S(1)}, f32[512,128]{1,0:T(8,128)}, u32[]{:S(2)}) copy-start(f32[512,128]{1,0:T(8,128)} %constant.33.clone) | copy-start | bytes 786436
  60.1 1.7 %copy-start.7 = (f32[2,128,256,1]{2,1,0,3:T(8,128)S(1)}, f32[2,128,256,1]{2,1,0,3:T(8,128)}, u32[]{:S(2)}) copy-start(f32[2,128,256,1]{2,1,0,3:T(8,128)} %constant.42) | copy-start | bytes 786436
  64.8 1.0 copy-start.9
  71.8 1.0 copy-start.3
  71.8 1.0 copy-start.4
  75.6 1.6 %copy-start.2 = (f32[512,1024]{1,0:T(8,128)S(1)}, f32[512,1024]{1,0:T(8,128)}, u32[]{:S(2)}) copy-start(f32[512,1024]{1,0:T(8,128)} %constant.35.clone) | copy-start | bytes 6291460

commit v2 on v1

v2 whole, which is shorter than its diff:
```python
import functools
import math

import jax
import jax.numpy as jnp
import numpy as np
from jax import lax
from jax.experimental import pallas as pl
from jax.experimental.pallas import tpu as pltpu
from jax.sharding import PartitionSpec as P

LANES = 128
SUB = 8
MESH = pl.DeviceIdType.MESH
COT, SIG, TAP, GRAD, FILT, INP = range(6)
KINDS = 6


def split_high_low(table):
    high = np.asarray(table, np.float32).astype(jnp.bfloat16)
    low = (table - high.astype(np.float64)).astype(np.float32).astype(jnp.bfloat16)
    return np.stack([high, low])


def tables(length):
    rows = length // LANES
    row_index = np.arange(rows)
    lane_index = np.arange(LANES)
    row_angle = ((4 * row_index[:, None] + 1) * row_index[None, :] % (4 * rows)) * (2.0 * math.pi / (4 * rows))
    twist_angle = ((4 * row_index[:, None] + 1) * lane_index[None, :] % (4 * length)) * (2.0 * math.pi / (4 * length))
    lane_angle = (lane_index[:, None] * lane_index[None, :] % LANES) * (2.0 * math.pi / LANES)
    row_forward = np.concatenate([np.cos(row_angle), -np.sin(row_angle)], axis=0)
    lane_cos, lane_sin = np.cos(lane_angle), np.sin(lane_angle)
    lane_forward = np.block([[lane_cos, -lane_sin], [lane_sin, lane_cos]])
    lane_inverse = np.block([[lane_cos, lane_sin], [-lane_sin, lane_cos]])
    return (
        split_high_low(row_forward),
        split_high_low(row_forward.T / length),
        np.concatenate([split_high_low(lane_forward), split_high_low(lane_inverse)], axis=0),
        np.stack([np.cos(twist_angle), np.sin(twist_angle)]).astype(np.float32),
    )


def dot(left, right):
    return jnp.dot(left, right, preferred_element_type=jnp.float32)


def dot_three(left, high, low):
    left_high = left.astype(jnp.bfloat16)
    left_low = (left - left_high.astype(jnp.float32)).astype(jnp.bfloat16)
    return dot(left_high, high) + (dot(left_low, high) + dot(left_high, low))


def kernel(
    members, devices,
    signal_ref, cot_ref, taps_ref, proj_ref, forward_hbm, inverse_hbm, lane_hbm, twist_hbm,
    input_out, filter_out,
    forward, inverse, lane, twist, work, cots,
    signal_send, taps_send, grad_send, filter_send, input_send,
    signal_got, taps_got, grad_got, filter_got, input_got,
    spectra, send_sem, recv_sem, table_sem,
):
    member = lax.axis_index("rep")
    place = lax.axis_index("seq")
    half = lax.axis_index("chan")
    owners = members * devices
    me = member * devices + place
    rows = devices * SUB
    width = signal_ref.shape[1]
    chunk = signal_ref.shape[0] // SUB

    barrier = pltpu.get_barrier_semaphore()

    def target(step):
        other = lax.rem(me + step, owners)
        return other, {"rep": other // devices, "seq": lax.rem(other, devices)}

    def greet(step, carry):
        pl.semaphore_signal(barrier, inc=1, device_id=target(step)[1], device_id_type=MESH)
        return carry

    lax.fori_loop(1, owners, greet, 0)
    partner = {"chan": 1 - half}
    pl.semaphore_signal(barrier, inc=1, device_id=partner, device_id_type=MESH)

    table_copies = [
        pltpu.make_async_copy(source, target_ref, table_sem.at[at])
        for at, (source, target_ref) in enumerate(
            ((forward_hbm, forward), (lane_hbm, lane), (twist_hbm, twist), (inverse_hbm, inverse))
        )
    ]
    for copy in table_copies:
        copy.start()

    def spread(source, target_ref):
        for j in range(SUB):
            work[pl.ds(j, width, stride=SUB), :] = source(j)
        target_ref[...] = work[...].reshape(width, SUB, LANES).astype(jnp.bfloat16)

    def block_of(ref):
        return lambda j: ref[j * chunk : (j + 1) * chunk, :].astype(jnp.float32).T

    spread(block_of(taps_ref), taps_send)
    spread(block_of(signal_ref), signal_send)
    pl.semaphore_wait(barrier, owners)

    cot_copy = pltpu.make_async_remote_copy(
        src_ref=cot_ref, dst_ref=cots.at[half], send_sem=send_sem.at[COT], recv_sem=recv_sem.at[COT],
        device_id=partner, device_id_type=MESH,
    )
    cot_copy.start()

    def exchange(kind, send_ref, got_ref):
        def send(step, carry):
            other, place_of = target(step)
            pltpu.make_async_remote_copy(
                src_ref=send_ref.at[other], dst_ref=got_ref.at[me],
                send_sem=send_sem.at[kind], recv_sem=recv_sem.at[kind],
                device_id=place_of, device_id_type=MESH,
            ).start()
            return carry

        lax.fori_loop(1, owners, send, 0)
        pltpu.make_async_copy(send_ref.at[me], got_ref.at[me], recv_sem.at[kind]).start()

    def arrived(kind, got_ref):
        pltpu.make_async_copy(got_ref, got_ref, recv_sem.at[kind]).wait()

    def sent(kind, send_ref, count):
        part = send_ref.at[pl.ds(0, count)]
        pltpu.make_async_copy(part, part, send_sem.at[kind]).wait()

    def send_taps(step, carry):
        other = lax.rem(place + step, devices)
        pltpu.make_async_remote_copy(
            src_ref=taps_send.at[member * devices + other], dst_ref=taps_got.at[place],
            send_sem=send_sem.at[TAP], recv_sem=recv_sem.at[TAP],
            device_id={"seq": other}, device_id_type=MESH,
        ).start()
        return carry

    lax.fori_loop(1, devices, send_taps, 0)
    pltpu.make_async_copy(taps_send.at[me], taps_got.at[place], recv_sem.at[TAP]).start()
    exchange(SIG, signal_send, signal_got)

    cots[half] = cot_ref[...]
    cot_copy.wait()

    def mixed(j):
        total = None
        for part in range(2):
            term = lax.dot_general(
                proj_ref[:, part * width : (part + 1) * width],
                cots[part, j * chunk : (j + 1) * chunk, :],
                (((1,), (1,)), ((), ())),
                preferred_element_type=jnp.float32,
            )
            total = term if total is None else total + term
        return total

    spread(mixed, grad_send)
    exchange(GRAD, grad_send, grad_got)

    for copy in table_copies:
        copy.wait()

    def transform(values, first):
        outer = dot(forward[0], values) + dot(forward[1], values)
        for at in range(values.shape[1] // LANES):
            real = outer[:rows, at * LANES : (at + 1) * LANES]
            imag = outer[rows:, at * LANES : (at + 1) * LANES]
            twisted = jnp.concatenate(
                [real * twist[0] + imag * twist[1], imag * twist[0] - real * twist[1]], axis=1
            )
            spectra[first + at] = dot_three(twisted, lane[0], lane[1])

    def member_rows(ref, at):
        return ref[at * devices : (at + 1) * devices].reshape(rows, LANES)

    def gathered(ref):
        return jnp.concatenate([member_rows(ref, at) for at in range(members)], axis=1)

    arrived(TAP, taps_got)
    arrived(SIG, signal_got)
    transform(jnp.concatenate([gathered(signal_got), taps_got[...].reshape(rows, LANES)], axis=1), 0)
    arrived(GRAD, grad_got)
    transform(gathered(grad_got), 3)

    def conj_product(first, second):
        first_real, first_imag = spectra[first, :, :LANES], spectra[first, :, LANES:]
        second_real, second_imag = spectra[second, :, :LANES], spectra[second, :, LANES:]
        return (
            first_real * second_real + first_imag * second_imag,
            first_imag * second_real - first_real * second_imag,
        )

    def untransform(pair):
        inner = dot_three(jnp.concatenate(pair, axis=1), lane[2], lane[3])
        real, imag = inner[:, :LANES], inner[:, LANES:]
        return jnp.concatenate(
            [real * twist[0] - imag * twist[1], imag * twist[0] + real * twist[1]], axis=0
        )

    def rows_inverse(values):
        high = values.astype(jnp.bfloat16)
        low = (values - high.astype(jnp.float32)).astype(jnp.bfloat16)
        return dot(inverse[0], high) + (dot(inverse[0], low) + dot(inverse[1], high))

    filter_terms = [conj_product(3 + at, at) for at in range(2)]
    filter_pair = tuple(first + second for first, second in zip(*filter_terms))
    filter_rows = rows_inverse(untransform(filter_pair)).astype(jnp.bfloat16).reshape(devices, SUB, LANES)
    for at in range(members):
        filter_send[at * devices : (at + 1) * devices] = filter_rows
    exchange(FILT, filter_send, filter_got)

    input_rows = rows_inverse(
        jnp.concatenate([untransform(conj_product(3 + at, 2)) for at in range(2)], axis=1)
    ).astype(jnp.bfloat16)
    for at in range(members):
        input_send[at * devices : (at + 1) * devices] = input_rows[
            :, at * LANES : (at + 1) * LANES
        ].reshape(devices, SUB, LANES)
    exchange(INP, input_send, input_got)

    def collect(got_ref, out_ref):
        work[...] = got_ref[...].astype(jnp.float32).reshape(width * SUB, LANES)
        for j in range(SUB):
            out_ref[j * chunk : (j + 1) * chunk, :] = work[pl.ds(j, width, stride=SUB), :].T.astype(
                out_ref.dtype
            )

    sent(TAP, taps_send, devices - 1)
    sent(SIG, signal_send, owners - 1)
    sent(GRAD, grad_send, owners - 1)
    arrived(FILT, filter_got)
    collect(filter_got, filter_out)
    arrived(INP, input_got)
    collect(input_got, input_out)
    sent(FILT, filter_send, owners - 1)
    sent(INP, input_send, owners - 1)


def per_device(inputs, cotangent, filter_taps, out_proj):
    devices = lax.axis_size("seq")
    members = lax.axis_size("rep")
    tok_rows, width = filter_taps.shape
    owners = members * devices
    rows = devices * SUB
    constants = [jnp.asarray(table) for table in tables(devices * tok_rows)]
    vmem = pl.BlockSpec(memory_space=pltpu.VMEM)
    hbm = pl.BlockSpec(memory_space=pl.ANY)
    message = (owners, SUB, LANES)
    grad_input, grad_filter = pl.pallas_call(
        functools.partial(kernel, members, devices),
        out_shape=(
            jax.ShapeDtypeStruct((tok_rows, width), jnp.bfloat16),
            jax.ShapeDtypeStruct((tok_rows, width), jnp.float32),
        ),
        in_specs=[vmem] * 4 + [hbm] * 4,
        out_specs=(vmem, vmem),
        scratch_shapes=[pltpu.VMEM(table.shape, table.dtype) for table in constants]
        + [
            pltpu.VMEM((width * SUB, LANES), jnp.float32),
            pltpu.VMEM((2, tok_rows, width), jnp.bfloat16),
        ]
        + [pltpu.VMEM(message, jnp.bfloat16)] * 5
        + [
            pltpu.VMEM(message, jnp.bfloat16),
            pltpu.VMEM((devices, SUB, LANES), jnp.bfloat16),
            pltpu.VMEM(message, jnp.bfloat16),
            pltpu.VMEM(message, jnp.bfloat16),
            pltpu.VMEM(message, jnp.bfloat16),
            pltpu.VMEM((5, rows, 2 * LANES), jnp.float32),
            pltpu.SemaphoreType.DMA((KINDS,)),
            pltpu.SemaphoreType.DMA((KINDS,)),
            pltpu.SemaphoreType.DMA((4,)),
        ],
        compiler_params=pltpu.CompilerParams(
            collective_id=0, has_side_effects=True, vmem_limit_bytes=48 * 1024 * 1024
        ),
        name="correlate",
    )(
        inputs.reshape(tok_rows, width),
        cotangent.reshape(tok_rows, width),
        filter_taps,
        out_proj,
        *constants,
    )
    return (grad_input.reshape(1, tok_rows, width), grad_filter)


def solution(mesh):
    return jax.shard_map(
        per_device,
        mesh=mesh,
        in_specs=(
            P("rep", "seq", "chan"),
            P("rep", "seq", "chan"),
            P("seq", "chan"),
            P("chan", None),
        ),
        out_specs=(P("rep", "seq", "chan"), P("seq", "chan")),
        check_vma=False,
    )
```

time: 114 us -> 64.5 us (0.57)
  blocking collectives: 71.4 us -> 0 us
  Pallas kernels: 0 us -> 54.7 us
  matrix products: 12.2 us -> 0 us
  other arithmetic: 10 us -> 0 us
  local copies, waits for them, and re-layouts: 18.7 us -> 8.85 us
    all_to_all x2 -> x0, blocking collectives: 61.6 us -> none  [per_device(): lax.all_to_all(outgoing, ('rep', 'seq'), split_axis=0, concat_axis=0, til...]
    pallas_call x0 -> x1, Pallas kernels: none -> 54.7 us  [per_device(): pl.pallas_call(functools.partial(kernel, members, devices), out_shape=(ja...]
    dot_general x5 -> x0, matrix products: 12.2 us -> none  [the longest x4 11.9 us: product(): jnp.dot(left, right, precision=precise_mode, preferred_element_type=jnp.f...]
    all_gather x1 -> x0, blocking collectives: 9.8 us -> none  [per_device(): lax.all_gather(cotangent.reshape(tok_rows, chan_width), 'chan', axis=1, t...]
    all_to_all x3 -> x0, other arithmetic: 4.85 us -> none  [per_device(): lax.all_to_all(outgoing, ('rep', 'seq'), split_axis=0, concat_axis=0, til...]
    squeeze x2 -> x0, local copies, waits for them, and re-layouts: 2.96 us -> none  [the longest x1 1.49 us: correlate(): outer[1] * sine]
    add x3 -> x0, other arithmetic: 1.97 us -> none  [the longest x1 1.66 us: correlate(): outer[0] * cosine + outer[1] * sine]
    unnamed x33 -> x16, local copies, waits for them, and re-layouts: 10.8 us -> 8.85 us
where the time goes in v2:
time: 64.5 us; the launch traced here: 64.2 us
  Pallas kernels  54.7 us (85%)
  local copies, waits for them, and re-layouts  8.85 us (14%)
  between operations  0.65 us (1%)
    pallas_call x1, Pallas kernels, per_device(): pl.pallas_call(functools.partial(kernel, members, devices), out_shape=(ja...  54.7 us
    unnamed x16, local copies, waits for them, and re-layouts  8.85 us

profile of v2, /device:TPU:1, one launch (start us, length us, event | category | flops | bytes accessed | tf_op | source)
XLA Modules:
  0.0 64.2 jit_solution(3074337390831866451)
XLA Ops:
  0.6 0.0 copy-start
  0.6 1.6 %copy-done = bf16[2,1024,512]{2,1,0:T(8,128)(2,1)S(1)} copy-done((bf16[2,1024,512]{2,1,0:T(8,128)(2,1)S(1)}, bf16[2,1024,512]{2,1,0:T(8,128)(2,1)}, u32[]{:S(2)}) %copy-start) | copy-done | bytes 2097176
  2.2 0.0 copy-start.1
  2.2 1.0 %copy-done.1 = f32[2,512,128]{2,1,0:T(8,128)S(1)} copy-done((f32[2,512,128]{2,1,0:T(8,128)S(1)}, f32[2,512,128]{2,1,0:T(8,128)}, u32[]{:S(2)}) %copy-start.1) | copy-done | bytes 524312
  3.3 0.0 copy-start.2
  3.3 1.0 %copy-done.2 = bf16[4,256,256]{2,1,0:T(8,128)(2,1)S(1)} copy-done((bf16[4,256,256]{2,1,0:T(8,128)(2,1)S(1)}, bf16[4,256,256]{2,1,0:T(8,128)(2,1)}, u32[]{:S(2)}) %copy-start.2) | copy-done | bytes 524312
  4.3 0.0 copy-start.3
  4.3 0.9 %copy-done.3 = bf16[1,1024,128]{2,1,0:T(8,128)(2,1)S(1)} copy-done((bf16[1,1024,128]{2,1,0:T(8,128)(2,1)S(1)}, bf16[1,1024,128]{2,1,0:T(8,128)(2,1)}, u32[]{:S(2)}) %copy-start.3) | copy-done | bytes 262168
  5.3 0.0 copy-start.4
  5.3 0.9 %copy-done.4 = bf16[1,1024,128]{2,1,0:T(8,128)(2,1)S(1)} copy-done((bf16[1,1024,128]{2,1,0:T(8,128)(2,1)S(1)}, bf16[1,1024,128]{2,1,0:T(8,128)(2,1)}, u32[]{:S(2)}) %copy-start.4) | copy-done | bytes 262168
  6.2 0.0 copy-start.5
  6.2 0.9 %copy-done.5 = bf16[1024,128]{1,0:T(8,128)(2,1)S(1)} copy-done((bf16[1024,128]{1,0:T(8,128)(2,1)S(1)}, bf16[1024,128]{1,0:T(8,128)(2,1)}, u32[]{:S(2)}) %copy-start.5) | copy-done | bytes 262168
  7.2 0.0 copy-start.6
  7.2 0.8 %copy-done.6 = bf16[128,256]{1,0:T(8,128)(2,1)S(1)} copy-done((bf16[128,256]{1,0:T(8,128)(2,1)S(1)}, bf16[128,256]{1,0:T(8,128)(2,1)}, u32[]{:S(2)}) %copy-start.6) | copy-done | bytes 65560
  8.0 54.7 %correlate.1 = (bf16[1024,128]{1,0:T(8,128)(2,1)S(1)}, f32[1024,128]{1,0:T(8,128)S(1)}) custom-call(bf16[1024,128]{1,0:T(8,128)(2,1)S(1)} %bitcast.3, bf16[1024,128]{1,0:T(8,128)(2,1)S(1)} %bitcast.4, bf16[1024,128]{1,0:T(8,128)(2,1)S(1)} %copy-done.5, bf16[128,256]{1,0:T(8,128)(2,1)S(1)} %copy-done.6, bf16[2,1024,512]{2,1,0:T(8,128)(2,1)S(1)} %copy-done, ...), custom_call_target="tpu_custom_call" | custom-call | tf_op jit(solution)/shard_map/correlate/pallas_call | solution.py:253
  62.7 0.7 %copy.12 = bf16[1,1024,128]{2,1,0:T(8,128)(2,1)} copy(bf16[1,1024,128]{2,1,0:T(8,128)(2,1)S(1)} %bitcast.5) | data formatting | bytes 524288
  63.4 0.8 %copy.13 = f32[1024,128]{1,0:T(8,128)} copy(f32[1024,128]{1,0:T(8,128)S(1)} %get-tuple-element.9) | data formatting | bytes 1048576
Async XLA Ops:
  0.6 1.6 %copy-start = (bf16[2,1024,512]{2,1,0:T(8,128)(2,1)S(1)}, bf16[2,1024,512]{2,1,0:T(8,128)(2,1)}, u32[]{:S(2)}) copy-start(bf16[2,1024,512]{2,1,0:T(8,128)(2,1)} %constant.8.clone.forward_hbm) | copy-start | bytes 6291460
  2.2 1.0 %copy-start.1 = (f32[2,512,128]{2,1,0:T(8,128)S(1)}, f32[2,512,128]{2,1,0:T(8,128)}, u32[]{:S(2)}) copy-start(f32[2,512,128]{2,1,0:T(8,128)} %constant.11.clone.twist_hbm) | copy-start | bytes 1572868
  3.3 1.0 %copy-start.2 = (bf16[4,256,256]{2,1,0:T(8,128)(2,1)S(1)}, bf16[4,256,256]{2,1,0:T(8,128)(2,1)}, u32[]{:S(2)}) copy-start(bf16[4,256,256]{2,1,0:T(8,128)(2,1)} %constant.10.clone.lane_hbm) | copy-start | bytes 1572868
  4.3 0.9 %copy-start.3 = (bf16[1,1024,128]{2,1,0:T(8,128)(2,1)S(1)}, bf16[1,1024,128]{2,1,0:T(8,128)(2,1)}, u32[]{:S(2)}) copy-start(bf16[1,1024,128]{2,1,0:T(8,128)(2,1)} %param.8) | copy-start | bytes 786436
  5.3 0.9 %copy-start.4 = (bf16[1,1024,128]{2,1,0:T(8,128)(2,1)S(1)}, bf16[1,1024,128]{2,1,0:T(8,128)(2,1)}, u32[]{:S(2)}) copy-start(bf16[1,1024,128]{2,1,0:T(8,128)(2,1)} %param.9) | copy-start | bytes 786436
  6.2 0.9 %copy-start.5 = (bf16[1024,128]{1,0:T(8,128)(2,1)S(1)}, bf16[1024,128]{1,0:T(8,128)(2,1)}, u32[]{:S(2)}) copy-start(bf16[1024,128]{1,0:T(8,128)(2,1)} %taps_ref.1) | copy-start | bytes 786436
  7.2 0.8 %copy-start.6 = (bf16[128,256]{1,0:T(8,128)(2,1)S(1)}, bf16[128,256]{1,0:T(8,128)(2,1)}, u32[]{:S(2)}) copy-start(bf16[128,256]{1,0:T(8,128)(2,1)} %proj_ref.1) | copy-start | bytes 196612

commit v3 on v2

v3 whole, which is shorter than its diff:
```python
import functools
import math

import jax
import jax.numpy as jnp
import numpy as np
from jax import lax
from jax.experimental import pallas as pl
from jax.experimental.pallas import tpu as pltpu
from jax.sharding import PartitionSpec as P

LANES = 128
SUB = 8
STEP = 128
WAVES = 8
VMEM_LIMIT = 60 * 1024 * 1024
MESH = pl.DeviceIdType.MESH
COT, SIG, TAP, GRAD, FILT, INP, SWAP = range(7)
KINDS = 7


def split_high_low(table):
    high = np.asarray(table, np.float32).astype(jnp.bfloat16)
    low = (table - high.astype(np.float64)).astype(np.float32).astype(jnp.bfloat16)
    return np.stack([high, low])


def tables(length):
    rows = length // LANES
    row_index = np.arange(rows)
    lane_index = np.arange(LANES)
    row_angle = ((4 * row_index[:, None] + 1) * row_index[None, :] % (4 * rows)) * (2.0 * math.pi / (4 * rows))
    twist_angle = ((4 * row_index[:, None] + 1) * lane_index[None, :] % (4 * length)) * (2.0 * math.pi / (4 * length))
    lane_angle = (lane_index[:, None] * lane_index[None, :] % LANES) * (2.0 * math.pi / LANES)
    row_forward = np.concatenate([np.cos(row_angle), -np.sin(row_angle)], axis=0)
    lane_cos, lane_sin = np.cos(lane_angle), np.sin(lane_angle)
    lane_forward = np.block([[lane_cos, -lane_sin], [lane_sin, lane_cos]])
    lane_inverse = np.block([[lane_cos, lane_sin], [-lane_sin, lane_cos]])
    forward_high, forward_low = split_high_low(row_forward)
    lane_tables = []
    for table in (lane_forward, lane_inverse):
        high, low = split_high_low(table)
        lane_tables.append(np.concatenate([high, high, low], axis=0))
    return (
        np.concatenate([forward_high, forward_low], axis=1),
        split_high_low(row_forward.T / length),
        np.stack(lane_tables),
        np.stack([np.cos(twist_angle), np.sin(twist_angle)]).astype(np.float32),
    )


def dot(left, right):
    return jnp.dot(left, right, preferred_element_type=jnp.float32)


def transposed(block):
    at_row = lax.broadcasted_iota(jnp.int32, block.shape, 0)
    at_lane = lax.broadcasted_iota(jnp.int32, block.shape, 1)
    identity = jnp.where(at_row == at_lane, 1.0, 0.0).astype(jnp.bfloat16)
    return block.astype(jnp.float32).T


def store_split(ref, slot, at_rows, at_lanes, value):
    high = value.astype(jnp.bfloat16)
    ref[2 * slot, at_rows, at_lanes] = high
    ref[2 * slot + 1, at_rows, at_lanes] = (value - high.astype(jnp.float32)).astype(jnp.bfloat16)


def kernel(
    members, devices,
    signal_hbm, cot_hbm, taps_hbm, proj_hbm, forward_hbm, inverse_hbm, lane_hbm, twist_hbm,
    input_got, filter_mid,
    forward, inverse, lane, twist, work, cots, signal_ref, taps_ref, proj_ref,
    signal_send, taps_send, grad_send, filter_send, input_send,
    signal_got, taps_got, grad_got, filter_got, filter_rows,
    outer, pieces, untwisted, spectra, send_sem, recv_sem, load_sem,
):
    member = lax.axis_index("rep")
    place = lax.axis_index("seq")
    half = lax.axis_index("chan")
    owners = members * devices
    me = member * devices + place
    rows = devices * SUB
    width = signal_ref.shape[1]
    chunk = signal_ref.shape[0] // SUB

    def device(owner, part):
        return {"rep": owner // devices, "seq": lax.rem(owner, devices), "chan": part}

    partner = device(me, 1 - half)
    sibling = (1 - member) * devices + place

    barrier = pltpu.get_barrier_semaphore()

    def others(body):
        def step(at, carry):
            body(lax.rem(me + at, owners))
            return carry

        lax.fori_loop(1, owners, step, 0)

    def others_of_member(body):
        def step(at, carry):
            body(lax.rem(place + at, devices))
            return carry

        lax.fori_loop(1, devices, step, 0)

    def others_in_waves(body):
        turns = owners // WAVES
        turn = me // WAVES
        for wave in range(WAVES):
            def step(at, carry):
                body(lax.rem(turn + at, turns) * WAVES + wave)
                return carry

            lax.fori_loop(1, turns, step, 0)

            @pl.when(lax.rem(me, WAVES) != wave)
            def _():
                body(turn * WAVES + wave)

    def greet(target):
        pl.semaphore_signal(barrier, inc=1, device_id=target, device_id_type=MESH)

    greet(partner)
    others(lambda owner: greet(device(owner, half)))

    loads = [
        pltpu.make_async_copy(source, target_ref, load_sem.at[at])
        for at, (source, target_ref) in enumerate(
            (
                (taps_hbm, taps_ref),
                (signal_hbm, signal_ref),
                (cot_hbm, cots.at[half]),
                (proj_hbm, proj_ref),
                (forward_hbm, forward),
                (lane_hbm, lane),
                (twist_hbm, twist),
                (inverse_hbm, inverse),
            )
        )
    ]
    for copy in loads:
        copy.start()

    def spread(source, target_ref):
        for j in range(SUB):
            work[pl.ds(j, width, stride=SUB), :] = source(j)
        target_ref[...] = work[...].reshape(width, SUB, LANES).astype(jnp.bfloat16)

    def block_of(ref):
        return lambda j: transposed(ref[j * chunk : (j + 1) * chunk, :])

    loads[0].wait()
    spread(block_of(taps_ref), taps_send)
    loads[1].wait()
    spread(block_of(signal_ref), signal_send)
    loads[2].wait()
    pl.semaphore_wait(barrier, owners)

    def remote(kind, source, target_ref, target):
        return pltpu.make_async_remote_copy(
            src_ref=source, dst_ref=target_ref, send_sem=send_sem.at[kind], recv_sem=recv_sem.at[kind],
            device_id=target, device_id_type=MESH,
        )

    cot_copy = remote(COT, cots.at[half], cots.at[half], partner)
    cot_copy.start()

    def exchange(kind, send_ref, got_ref, order=others):
        order(lambda owner: remote(kind, send_ref.at[owner], got_ref.at[me], device(owner, half)).start())
        pltpu.make_async_copy(send_ref.at[me], got_ref.at[me], recv_sem.at[kind]).start()

    def arrived(kind, got_ref):
        pltpu.make_async_copy(got_ref, got_ref, recv_sem.at[kind]).wait()

    def sent(kind, send_ref, count):
        part = send_ref.at[pl.ds(0, count)]
        pltpu.make_async_copy(part, part, send_sem.at[kind]).wait()

    others_of_member(
        lambda other: remote(
            TAP, taps_send.at[member * devices + other], taps_got.at[place], device(member * devices + other, half)
        ).start()
    )
    pltpu.make_async_copy(taps_send.at[me], taps_got.at[place], recv_sem.at[TAP]).start()
    exchange(SIG, signal_send, signal_got)

    loads[3].wait()
    cot_copy.wait_recv()

    def mixed(j):
        total = None
        for part in range(2):
            term = lax.dot_general(
                proj_ref[:, part * width : (part + 1) * width],
                cots[part, j * chunk : (j + 1) * chunk, :],
                (((1,), (1,)), ((), ())),
                preferred_element_type=jnp.float32,
            )
            total = term if total is None else total + term
        return total

    spread(mixed, grad_send)
    exchange(GRAD, grad_send, grad_got, others_in_waves)

    for copy in loads[4:]:
        copy.wait()

    steps = [slice(at, at + STEP) for at in range(0, rows, STEP)]
    lower = [slice(rows + at, rows + at + STEP) for at in range(0, rows, STEP)]
    real_lanes, imag_lanes = slice(0, LANES), slice(LANES, 2 * LANES)

    def lane_dot(slot, table):
        high, low = pieces[2 * slot], pieces[2 * slot + 1]
        return dot(jnp.concatenate([high, low, high], axis=1), lane[table])

    def transform(values, first):
        count = values.shape[1] // LANES
        outer[:, : count * LANES] = dot(forward[...], jnp.concatenate([values, values], axis=0))
        for at in range(count):
            lanes = slice(at * LANES, (at + 1) * LANES)
            slot = at % 2
            for upper_rows, lower_rows in zip(steps, lower):
                real, imag = outer[upper_rows, lanes], outer[lower_rows, lanes]
                cosine, sine = twist[0, upper_rows], twist[1, upper_rows]
                store_split(pieces, slot, upper_rows, real_lanes, real * cosine + imag * sine)
                store_split(pieces, slot, upper_rows, imag_lanes, imag * cosine - real * sine)
            spectra[first + at] = lane_dot(slot, 0)

    def member_rows(ref, at):
        return ref[at * devices : (at + 1) * devices].reshape(rows, LANES)

    def gathered(ref):
        return jnp.concatenate([member_rows(ref, at) for at in range(members)], axis=1)

    arrived(TAP, taps_got)
    arrived(SIG, signal_got)
    transform(jnp.concatenate([gathered(signal_got), taps_got[...].reshape(rows, LANES)], axis=1), 0)
    arrived(GRAD, grad_got)
    transform(gathered(grad_got), 3)

    def conj_product(pairs, at_rows):
        real_total = imag_total = None
        for first, second in pairs:
            first_real, first_imag = spectra[first, at_rows, real_lanes], spectra[first, at_rows, imag_lanes]
            second_real, second_imag = spectra[second, at_rows, real_lanes], spectra[second, at_rows, imag_lanes]
            real = first_real * second_real + first_imag * second_imag
            imag = first_imag * second_real - first_real * second_imag
            real_total = real if real_total is None else real_total + real
            imag_total = imag if imag_total is None else imag_total + imag
        return real_total, imag_total

    def untransform(pairs, slot, lanes):
        for upper_rows in steps:
            real, imag = conj_product(pairs, upper_rows)
            store_split(pieces, slot, upper_rows, real_lanes, real)
            store_split(pieces, slot, upper_rows, imag_lanes, imag)
        outer[:rows, : 2 * LANES] = lane_dot(slot, 1)
        for upper_rows, lower_rows in zip(steps, lower):
            real, imag = outer[upper_rows, real_lanes], outer[upper_rows, imag_lanes]
            cosine, sine = twist[0, upper_rows], twist[1, upper_rows]
            store_split(untwisted, 0, upper_rows, lanes, real * cosine - imag * sine)
            store_split(untwisted, 0, lower_rows, lanes, imag * cosine + real * sine)

    def rows_inverse(lanes):
        high, low = untwisted[0, :, lanes], untwisted[1, :, lanes]
        table = jnp.concatenate([inverse[0], inverse[0], inverse[1]], axis=1)
        return dot(table, jnp.concatenate([high, low, high], axis=0)).astype(jnp.bfloat16)

    untransform(((3, 0), (4, 1)), 0, slice(0, LANES))
    filter_send[...] = rows_inverse(slice(0, LANES)).reshape(devices, SUB, LANES)
    others_of_member(
        lambda other: remote(
            FILT, filter_send.at[other], filter_got.at[member, place], device(member * devices + other, half)
        ).start()
    )
    pltpu.make_async_copy(filter_send.at[place], filter_got.at[member, place], recv_sem.at[FILT]).start()

    for at in range(members):
        untransform(((3 + at, 2),), 1 - at, slice((1 + at) * LANES, (2 + at) * LANES))
    input_rows = rows_inverse(slice(LANES, 3 * LANES))
    for at in range(members):
        input_send[at * devices : (at + 1) * devices] = input_rows[
            :, at * LANES : (at + 1) * LANES
        ].reshape(devices, SUB, LANES)
    exchange(INP, input_send, input_got)

    ours = filter_got.at[member]
    arrived(FILT, ours)
    swap = remote(SWAP, ours, ours, device(sibling, half))
    swap.start()
    cot_copy.wait_send()
    sent(TAP, taps_send, devices - 1)
    sent(SIG, signal_send, owners - 1)
    sent(GRAD, grad_send, owners - 1)
    sent(FILT, filter_send, devices - 1)
    swap.wait()
    work[...] = filter_got[...].astype(jnp.float32).reshape(width * SUB, LANES)
    for j in range(SUB):
        block = work[pl.ds(j, width, stride=SUB), :].astype(jnp.bfloat16)
        filter_rows[j * chunk : (j + 1) * chunk, :] = transposed(block).astype(jnp.bfloat16)
    keep = pltpu.make_async_copy(filter_rows, filter_mid, load_sem.at[0])
    keep.start()
    keep.wait()
    arrived(INP, input_got)
    sent(INP, input_send, owners - 1)


def finish_kernel(input_hbm, filter_hbm, input_out, filter_out, input_raw, filter_raw, work, input_done, filter_done, sems):
    copies = [
        pltpu.make_async_copy(source, target, sems.at[at])
        for at, (source, target) in enumerate(
            ((input_hbm, input_raw), (filter_hbm, filter_raw), (input_done, input_out), (filter_done, filter_out))
        )
    ]
    copies[0].start()
    copies[1].start()
    width = input_raw.shape[0]
    copies[1].wait()
    filter_done[...] = filter_raw[...].astype(jnp.float32)
    copies[3].start()
    copies[0].wait()
    work[...] = input_raw[...].astype(jnp.float32).reshape(work.shape)
    for j in range(SUB):
        block = work[pl.ds(j, width, stride=SUB), :].astype(jnp.bfloat16)
        input_done[j * LANES : (j + 1) * LANES, :] = transposed(block).astype(jnp.bfloat16)
    copies[2].start()
    copies[3].wait()
    copies[2].wait()


def per_device(inputs, cotangent, filter_taps, out_proj):
    devices = lax.axis_size("seq")
    members = lax.axis_size("rep")
    tok_rows, width = filter_taps.shape
    owners = members * devices
    rows = devices * SUB
    constants = [jnp.asarray(table) for table in tables(devices * tok_rows)]
    hbm = pl.BlockSpec(memory_space=pl.ANY)
    message = (owners, SUB, LANES)
    flat = (tok_rows, width)

    def buffers(shapes, dtype):
        return [pltpu.VMEM(shape, dtype) for shape in shapes]

    input_raw, filter_raw = pl.pallas_call(
        functools.partial(kernel, members, devices),
        out_shape=(jax.ShapeDtypeStruct(message, jnp.bfloat16), jax.ShapeDtypeStruct(flat, jnp.bfloat16)),
        in_specs=[hbm] * 8,
        out_specs=(hbm, hbm),
        scratch_shapes=[pltpu.VMEM(table.shape, table.dtype) for table in constants]
        + buffers([(width * SUB, LANES)], jnp.float32)
        + buffers(
            [(2, *flat), flat, flat, out_proj.shape]
            + [message] * 3
            + [(devices, SUB, LANES), message]
            + [message, (devices, SUB, LANES), message, (members, devices, SUB, LANES), flat],
            jnp.bfloat16,
        )
        + buffers([(2 * rows, 3 * LANES)], jnp.float32)
        + buffers([(4, rows, 2 * LANES), (2, 2 * rows, 3 * LANES)], jnp.bfloat16)
        + buffers([(5, rows, 2 * LANES)], jnp.float32)
        + [
            pltpu.SemaphoreType.DMA((KINDS,)),
            pltpu.SemaphoreType.DMA((KINDS,)),
            pltpu.SemaphoreType.DMA((8,)),
        ],
        compiler_params=pltpu.CompilerParams(
            collective_id=0, has_side_effects=True, vmem_limit_bytes=VMEM_LIMIT
        ),
        name="correlate",
    )(inputs.reshape(flat), cotangent.reshape(flat), filter_taps, out_proj, *constants)
    grad_input, grad_filter = pl.pallas_call(
        finish_kernel,
        out_shape=(jax.ShapeDtypeStruct(flat, jnp.bfloat16), jax.ShapeDtypeStruct(flat, jnp.float32)),
        in_specs=[hbm] * 2,
        out_specs=(hbm, hbm),
        scratch_shapes=buffers([message, flat], jnp.bfloat16)
        + buffers([(width * SUB, LANES)], jnp.float32)
        + buffers([flat], jnp.bfloat16)
        + buffers([flat], jnp.float32)
        + [pltpu.SemaphoreType.DMA((4,))],
        compiler_params=pltpu.CompilerParams(vmem_limit_bytes=VMEM_LIMIT),
        name="finish",
    )(input_raw, filter_raw)
    return (grad_input.reshape(1, tok_rows, width), grad_filter)


def solution(mesh):
    return jax.shard_map(
        per_device,
        mesh=mesh,
        in_specs=(
            P("rep", "seq", "chan"),
            P("rep", "seq", "chan"),
            P("seq", "chan"),
            P("chan", None),
        ),
        out_specs=(P("rep", "seq", "chan"), P("seq", "chan")),
        check_vma=False,
    )
```

time: 64.5 us -> 56.4 us (0.87)
  local copies, waits for them, and re-layouts: 8.85 us -> 0 us
  Pallas kernels: 54.7 us -> 55.7 us
    unnamed x16 -> x0, local copies, waits for them, and re-layouts: 8.85 us -> none
    pallas_call x0 -> x1, Pallas kernels: none -> 1.98 us  [per_device(): pl.pallas_call(finish_kernel, out_shape=(jax.ShapeDtypeStruct(flat, jnp.b...]
    pallas_call x1, Pallas kernels: 54.7 us -> 53.7 us  [per_device(): pl.pallas_call(functools.partial(kernel, members, devices), out_shape=(ja...]
where the time goes in v3:
time: 56.4 us; the launch traced here: 56.3 us
  Pallas kernels  55.7 us (99%)
  between operations  0.64 us (1%)
    pallas_call x1, Pallas kernels, per_device(): pl.pallas_call(functools.partial(kernel, members, devices), out_shape=(ja...  53.7 us
    pallas_call x1, Pallas kernels, per_device(): pl.pallas_call(finish_kernel, out_shape=(jax.ShapeDtypeStruct(flat, jnp.b...  1.98 us

profile of v3, /device:TPU:1, one launch (start us, length us, event | category | flops | bytes accessed | tf_op | source)
XLA Modules:
  0.0 56.3 jit_solution(3222947684525637783)
XLA Ops:
  0.6 53.7 %correlate.1 = (bf16[128,8,128]{2,1,0:T(8,128)(2,1)}, bf16[1024,128]{1,0:T(8,128)(2,1)}) custom-call(bf16[1024,128]{1,0:T(8,128)(2,1)} %bitcast.3, bf16[1024,128]{1,0:T(8,128)(2,1)} %bitcast.4, bf16[1024,128]{1,0:T(8,128)(2,1)} %taps_hbm.1, bf16[128,256]{1,0:T(8,128)(2,1)} %proj_hbm.1, bf16[1024,1024]{1,0:T(8,128)(2,1)} %constant.8.clone.forward_hbm, ...), custom_call_target="tpu_custom_call" | custom-call | tf_op jit(solution)/shard_map/correlate/pallas_call | solution.py:348
  54.4 2.0 %finish.1 = (bf16[1024,128]{1,0:T(8,128)(2,1)}, f32[1024,128]{1,0:T(8,128)}) custom-call(bf16[128,8,128]{2,1,0:T(8,128)(2,1)} %get-tuple-element.6.input_hbm, bf16[1024,128]{1,0:T(8,128)(2,1)} %get-tuple-element.7.filter_hbm), custom_call_target="tpu_custom_call" | custom-call | tf_op jit(solution)/shard_map/finish/pallas_call | solution.py:375

commit v4 on v3

--- a/solution.py
+++ b/solution.py
@@ -12,7 +12,7 @@
 LANES = 128
 SUB = 8
 STEP = 128
-WAVES = 8
+WAVES = 2
 VMEM_LIMIT = 60 * 1024 * 1024
 MESH = pl.DeviceIdType.MESH
 COT, SIG, TAP, GRAD, FILT, INP, SWAP = range(7)
@@ -43,7 +43,7 @@
         lane_tables.append(np.concatenate([high, high, low], axis=0))
     return (
         np.concatenate([forward_high, forward_low], axis=1),
-        split_high_low(row_forward.T / length),
+        np.concatenate(list(split_high_low(row_forward.T / length)), axis=1),
         np.stack(lane_tables),
         np.stack([np.cos(twist_angle), np.sin(twist_angle)]).astype(np.float32),
     )
@@ -84,47 +84,44 @@
     width = signal_ref.shape[1]
     chunk = signal_ref.shape[0] // SUB
 
-    def device(owner, part):
-        return {"rep": owner // devices, "seq": lax.rem(owner, devices), "chan": part}
-
-    partner = device(me, 1 - half)
-    sibling = (1 - member) * devices + place
+    other_member = 1 - member
+
+    def device(at_member, at_place, part):
+        return {"rep": at_member, "seq": at_place, "chan": part}
+
+    def around(start, count, first, body):
+        def step(at, carry):
+            body(lax.rem(start + at, count))
+            return carry
+
+        lax.fori_loop(first, count, step, 0)
 
     barrier = pltpu.get_barrier_semaphore()
 
     def others(body):
-        def step(at, carry):
-            body(lax.rem(me + at, owners))
-            return carry
-
-        lax.fori_loop(1, owners, step, 0)
+        around(place, devices, 1, lambda at_place: body(member, at_place))
+        around(place, devices, 0, lambda at_place: body(other_member, at_place))
 
     def others_of_member(body):
-        def step(at, carry):
-            body(lax.rem(place + at, devices))
-            return carry
-
-        lax.fori_loop(1, devices, step, 0)
+        around(place, devices, 1, body)
 
     def others_in_waves(body):
-        turns = owners // WAVES
-        turn = me // WAVES
+        turns = devices // WAVES
+        turn = place // WAVES
         for wave in range(WAVES):
-            def step(at, carry):
-                body(lax.rem(turn + at, turns) * WAVES + wave)
-                return carry
-
-            lax.fori_loop(1, turns, step, 0)
-
-            @pl.when(lax.rem(me, WAVES) != wave)
+            around(turn, turns, 1, lambda at: body(member, at * WAVES + wave))
+
+            @pl.when(lax.rem(place, WAVES) != wave)
             def _():
-                body(turn * WAVES + wave)
+                body(member, turn * WAVES + wave)
+
+            around(turn, turns, 0, lambda at: body(other_member, at * WAVES + wave))
 
     def greet(target):
         pl.semaphore_signal(barrier, inc=1, device_id=target, device_id_type=MESH)
 
-    greet(partner)
-    others(lambda owner: greet(device(owner, half)))
+    greet(device(member, place, 1 - half))
+    others(lambda at_member, at_place: greet(device(at_member, at_place, half)))
 
     loads = [
         pltpu.make_async_copy(source, target_ref, load_sem.at[at])
@@ -165,11 +162,15 @@
             device_id=target, device_id_type=MESH,
         )
 
-    cot_copy = remote(COT, cots.at[half], cots.at[half], partner)
+    cot_copy = remote(COT, cots.at[half], cots.at[half], device(member, place, 1 - half))
     cot_copy.start()
 
     def exchange(kind, send_ref, got_ref, order=others):
-        order(lambda owner: remote(kind, send_ref.at[owner], got_ref.at[me], device(owner, half)).start())
+        order(
+            lambda at_member, at_place: remote(
+                kind, send_ref.at[at_member * devices + at_place], got_ref.at[me], device(at_member, at_place, half)
+            ).start()
+        )
         pltpu.make_async_copy(send_ref.at[me], got_ref.at[me], recv_sem.at[kind]).start()
 
     def arrived(kind, got_ref):
@@ -181,7 +182,7 @@
 
     others_of_member(
         lambda other: remote(
-            TAP, taps_send.at[member * devices + other], taps_got.at[place], device(member * devices + other, half)
+            TAP, taps_send.at[member * devices + other], taps_got.at[place], device(member, other, half)
         ).start()
     )
     pltpu.make_async_copy(taps_send.at[me], taps_got.at[place], recv_sem.at[TAP]).start()
@@ -255,25 +256,25 @@
     def untransform(pairs, slot, lanes):
         for upper_rows in steps:
             real, imag = conj_product(pairs, upper_rows)
-            store_split(pieces, slot, upper_rows, real_lanes, real)
-            store_split(pieces, slot, upper_rows, imag_lanes, imag)
-        outer[:rows, : 2 * LANES] = lane_dot(slot, 1)
+            pieces[2 * slot, upper_rows, real_lanes] = real.astype(jnp.bfloat16)
+            pieces[2 * slot, upper_rows, imag_lanes] = imag.astype(jnp.bfloat16)
+        high = pieces[2 * slot]
+        outer[:rows, : 2 * LANES] = dot(jnp.concatenate([high, high], axis=1), lane[1, 2 * LANES :])
         for upper_rows, lower_rows in zip(steps, lower):
             real, imag = outer[upper_rows, real_lanes], outer[upper_rows, imag_lanes]
             cosine, sine = twist[0, upper_rows], twist[1, upper_rows]
-            store_split(untwisted, 0, upper_rows, lanes, real * cosine - imag * sine)
-            store_split(untwisted, 0, lower_rows, lanes, imag * cosine + real * sine)
+            untwisted[upper_rows, lanes] = (real * cosine - imag * sine).astype(jnp.bfloat16)
+            untwisted[lower_rows, lanes] = (imag * cosine + real * sine).astype(jnp.bfloat16)
 
     def rows_inverse(lanes):
-        high, low = untwisted[0, :, lanes], untwisted[1, :, lanes]
-        table = jnp.concatenate([inverse[0], inverse[0], inverse[1]], axis=1)
-        return dot(table, jnp.concatenate([high, low, high], axis=0)).astype(jnp.bfloat16)
+        values = untwisted[:, lanes]
+        return dot(inverse[...], jnp.concatenate([values, values], axis=0)).astype(jnp.bfloat16)
 
     untransform(((3, 0), (4, 1)), 0, slice(0, LANES))
     filter_send[...] = rows_inverse(slice(0, LANES)).reshape(devices, SUB, LANES)
     others_of_member(
         lambda other: remote(
-            FILT, filter_send.at[other], filter_got.at[member, place], device(member * devices + other, half)
+            FILT, filter_send.at[other], filter_got.at[member, place], device(member, other, half)
         ).start()
     )
     pltpu.make_async_copy(filter_send.at[place], filter_got.at[member, place], recv_sem.at[FILT]).start()
@@ -289,7 +290,7 @@
 
     ours = filter_got.at[member]
     arrived(FILT, ours)
-    swap = remote(SWAP, ours, ours, device(sibling, half))
+    swap = remote(SWAP, ours, ours, device(other_member, place, half))
     swap.start()
     cot_copy.wait_send()
     sent(TAP, taps_send, devices - 1)
@@ -360,7 +361,7 @@
             jnp.bfloat16,
         )
         + buffers([(2 * rows, 3 * LANES)], jnp.float32)
-        + buffers([(4, rows, 2 * LANES), (2, 2 * rows, 3 * LANES)], jnp.bfloat16)
+        + buffers([(4, rows, 2 * LANES), (2 * rows, 3 * LANES)], jnp.bfloat16)
         + buffers([(5, rows, 2 * LANES)], jnp.float32)
         + [
             pltpu.SemaphoreType.DMA((KINDS,)),

time: 56.4 us -> 54 us (0.957)
  Pallas kernels: 55.7 us -> 53.2 us
    pallas_call x1, Pallas kernels: 53.7 us -> 51.2 us  [per_device(): pl.pallas_call(functools.partial(kernel, members, devices), out_shape=(ja...]
where the time goes in v4:
time: 54 us; the launch traced here: 53.9 us
  Pallas kernels  53.2 us (99%)
  between operations  0.64 us (1%)
    pallas_call x1, Pallas kernels, per_device(): pl.pallas_call(functools.partial(kernel, members, devices), out_shape=(ja...  51.2 us
    pallas_call x1, Pallas kernels, per_device(): pl.pallas_call(finish_kernel, out_shape=(jax.ShapeDtypeStruct(flat, jnp.b...  1.98 us

profile of v4, /device:TPU:1, one launch (start us, length us, event | category | flops | bytes accessed | tf_op | source)
XLA Modules:
  0.0 53.9 jit_solution(14200084156660823463)
XLA Ops:
  0.6 51.2 %correlate.1 = (bf16[128,8,128]{2,1,0:T(8,128)(2,1)}, bf16[1024,128]{1,0:T(8,128)(2,1)}) custom-call(bf16[1024,128]{1,0:T(8,128)(2,1)} %bitcast.3, bf16[1024,128]{1,0:T(8,128)(2,1)} %bitcast.4, bf16[1024,128]{1,0:T(8,128)(2,1)} %taps_hbm.1, bf16[128,256]{1,0:T(8,128)(2,1)} %proj_hbm.1, bf16[1024,1024]{1,0:T(8,128)(2,1)} %constant.8.clone.forward_hbm, ...), custom_call_target="tpu_custom_call" | custom-call | tf_op jit(solution)/shard_map/correlate/pallas_call | solution.py:349
  51.9 2.0 %finish.1 = (bf16[1024,128]{1,0:T(8,128)(2,1)}, f32[1024,128]{1,0:T(8,128)}) custom-call(bf16[128,8,128]{2,1,0:T(8,128)(2,1)} %get-tuple-element.6.input_hbm, bf16[1024,128]{1,0:T(8,128)(2,1)} %get-tuple-element.7.filter_hbm), custom_call_target="tpu_custom_call" | custom-call | tf_op jit(solution)/shard_map/finish/pallas_call | solution.py:376

commit v5 on v4

--- a/solution.py
+++ b/solution.py
@@ -279,14 +279,17 @@
     )
     pltpu.make_async_copy(filter_send.at[place], filter_got.at[member, place], recv_sem.at[FILT]).start()
 
-    for at in range(members):
-        untransform(((3 + at, 2),), 1 - at, slice((1 + at) * LANES, (2 + at) * LANES))
-    input_rows = rows_inverse(slice(LANES, 3 * LANES))
-    for at in range(members):
-        input_send[at * devices : (at + 1) * devices] = input_rows[
-            :, at * LANES : (at + 1) * LANES
-        ].reshape(devices, SUB, LANES)
-    exchange(INP, input_send, input_got)
+    for turn in range(members):
+        at = other_member if turn else member
+        lanes = slice((1 + turn) * LANES, (2 + turn) * LANES)
+        untransform(((3 + at, 2),), 1 - turn, lanes)
+        input_send[pl.ds(at * devices, devices)] = rows_inverse(lanes).reshape(devices, SUB, LANES)
+
+        def send_input(at_place, at=at):
+            remote(INP, input_send.at[at * devices + at_place], input_got.at[me], device(at, at_place, half)).start()
+
+        around(place, devices, 0 if turn else 1, send_input)
+    pltpu.make_async_copy(input_send.at[me], input_got.at[me], recv_sem.at[INP]).start()
 
     ours = filter_got.at[member]
     arrived(FILT, ours)

time: 54 us -> 54.1 us (level)
  no operation moved by 1% of the time
where the time goes in v5:
time: 54.1 us; the launch traced here: 54 us
  Pallas kernels  53.3 us (99%)
  between operations  0.64 us (1%)
    pallas_call x1, Pallas kernels, per_device(): pl.pallas_call(functools.partial(kernel, members, devices), out_shape=(ja...  51.3 us
    pallas_call x1, Pallas kernels, per_device(): pl.pallas_call(finish_kernel, out_shape=(jax.ShapeDtypeStruct(flat, jnp.b...  1.98 us

profile of v5, /device:TPU:1, one launch (start us, length us, event | category | flops | bytes accessed | tf_op | source)
XLA Modules:
  0.0 54.0 jit_solution(3016466749813145597)
XLA Ops:
  0.6 51.3 %correlate.1 = (bf16[128,8,128]{2,1,0:T(8,128)(2,1)}, bf16[1024,128]{1,0:T(8,128)(2,1)}) custom-call(bf16[1024,128]{1,0:T(8,128)(2,1)} %bitcast.3, bf16[1024,128]{1,0:T(8,128)(2,1)} %bitcast.4, bf16[1024,128]{1,0:T(8,128)(2,1)} %taps_hbm.1, bf16[128,256]{1,0:T(8,128)(2,1)} %proj_hbm.1, bf16[1024,1024]{1,0:T(8,128)(2,1)} %constant.8.clone.forward_hbm, ...), custom_call_target="tpu_custom_call" | custom-call | tf_op jit(solution)/shard_map/correlate/pallas_call | solution.py:352
  52.0 2.0 %finish.1 = (bf16[1024,128]{1,0:T(8,128)(2,1)}, f32[1024,128]{1,0:T(8,128)}) custom-call(bf16[128,8,128]{2,1,0:T(8,128)(2,1)} %get-tuple-element.6.input_hbm, bf16[1024,128]{1,0:T(8,128)(2,1)} %get-tuple-element.7.filter_hbm), custom_call_target="tpu_custom_call" | custom-call | tf_op jit(solution)/shard_map/finish/pallas_call | solution.py:379

commit v6 on v5

--- a/solution.py
+++ b/solution.py
@@ -13,6 +13,7 @@
 SUB = 8
 STEP = 128
 WAVES = 2
+PARTS = 2
 VMEM_LIMIT = 60 * 1024 * 1024
 MESH = pl.DeviceIdType.MESH
 COT, SIG, TAP, GRAD, FILT, INP, SWAP = range(7)
@@ -69,10 +70,10 @@
 def kernel(
     members, devices,
     signal_hbm, cot_hbm, taps_hbm, proj_hbm, forward_hbm, inverse_hbm, lane_hbm, twist_hbm,
-    input_got, filter_mid,
+    input_got, filter_all,
     forward, inverse, lane, twist, work, cots, signal_ref, taps_ref, proj_ref,
     signal_send, taps_send, grad_send, filter_send, input_send,
-    signal_got, taps_got, grad_got, filter_got, filter_rows,
+    signal_got, taps_got, grad_got, filter_got,
     outer, pieces, untwisted, spectra, send_sem, recv_sem, load_sem,
 ):
     member = lax.axis_index("rep")
@@ -274,10 +275,10 @@
     filter_send[...] = rows_inverse(slice(0, LANES)).reshape(devices, SUB, LANES)
     others_of_member(
         lambda other: remote(
-            FILT, filter_send.at[other], filter_got.at[member, place], device(member, other, half)
+            FILT, filter_send.at[other], filter_got.at[place], device(member, other, half)
         ).start()
     )
-    pltpu.make_async_copy(filter_send.at[place], filter_got.at[member, place], recv_sem.at[FILT]).start()
+    pltpu.make_async_copy(filter_send.at[place], filter_got.at[place], recv_sem.at[FILT]).start()
 
     for turn in range(members):
         at = other_member if turn else member
@@ -291,48 +292,48 @@
         around(place, devices, 0 if turn else 1, send_input)
     pltpu.make_async_copy(input_send.at[me], input_got.at[me], recv_sem.at[INP]).start()
 
-    ours = filter_got.at[member]
-    arrived(FILT, ours)
-    swap = remote(SWAP, ours, ours, device(other_member, place, half))
+    arrived(FILT, filter_got)
+    swap = remote(SWAP, filter_got, filter_all.at[member], device(other_member, place, half))
     swap.start()
+    keep = pltpu.make_async_copy(filter_got, filter_all.at[member], load_sem.at[0])
+    keep.start()
     cot_copy.wait_send()
     sent(TAP, taps_send, devices - 1)
     sent(SIG, signal_send, owners - 1)
     sent(GRAD, grad_send, owners - 1)
     sent(FILT, filter_send, devices - 1)
+    keep.wait()
     swap.wait()
-    work[...] = filter_got[...].astype(jnp.float32).reshape(width * SUB, LANES)
-    for j in range(SUB):
-        block = work[pl.ds(j, width, stride=SUB), :].astype(jnp.bfloat16)
-        filter_rows[j * chunk : (j + 1) * chunk, :] = transposed(block).astype(jnp.bfloat16)
-    keep = pltpu.make_async_copy(filter_rows, filter_mid, load_sem.at[0])
-    keep.start()
-    keep.wait()
     arrived(INP, input_got)
     sent(INP, input_send, owners - 1)
 
 
-def finish_kernel(input_hbm, filter_hbm, input_out, filter_out, input_raw, filter_raw, work, input_done, filter_done, sems):
-    copies = [
-        pltpu.make_async_copy(source, target, sems.at[at])
-        for at, (source, target) in enumerate(
-            ((input_hbm, input_raw), (filter_hbm, filter_raw), (input_done, input_out), (filter_done, filter_out))
-        )
-    ]
-    copies[0].start()
-    copies[1].start()
+def finish_kernel(
+    input_hbm, filter_hbm, input_out, filter_out,
+    input_raw, filter_raw, input_work, filter_work, input_done, filter_done, load_sems, keep_sems,
+):
+    input_load = pltpu.make_async_copy(input_hbm, input_raw, load_sems.at[0])
+    filter_load = pltpu.make_async_copy(filter_hbm, filter_raw, load_sems.at[1])
+    filter_load.start()
+    input_load.start()
     width = input_raw.shape[0]
-    copies[1].wait()
-    filter_done[...] = filter_raw[...].astype(jnp.float32)
-    copies[3].start()
-    copies[0].wait()
-    work[...] = input_raw[...].astype(jnp.float32).reshape(work.shape)
-    for j in range(SUB):
-        block = work[pl.ds(j, width, stride=SUB), :].astype(jnp.bfloat16)
-        input_done[j * LANES : (j + 1) * LANES, :] = transposed(block).astype(jnp.bfloat16)
-    copies[2].start()
-    copies[3].wait()
-    copies[2].wait()
+    part_rows = input_out.shape[0] // PARTS
+    keeps = []
+    for load, raw, work, done, out in (
+        (filter_load, filter_raw, filter_work, filter_done, filter_out),
+        (input_load, input_raw, input_work, input_done, input_out),
+    ):
+        load.wait()
+        work[...] = raw[...].astype(jnp.float32).reshape(work.shape)
+        for j in range(SUB):
+            block = work[pl.ds(j, width, stride=SUB), :]
+            done[j * LANES : (j + 1) * LANES, :] = block.T.astype(done.dtype)
+            if (j + 1) * LANES % part_rows == 0:
+                part = pl.ds((j + 1) * LANES - part_rows, part_rows)
+                keeps.append(pltpu.make_async_copy(done.at[part], out.at[part], keep_sems.at[len(keeps)]))
+                keeps[-1].start()
+    for keep in keeps:
+        keep.wait()
 
 
 def per_device(inputs, cotangent, filter_taps, out_proj):
@@ -351,7 +352,10 @@
 
     input_raw, filter_raw = pl.pallas_call(
         functools.partial(kernel, members, devices),
-        out_shape=(jax.ShapeDtypeStruct(message, jnp.bfloat16), jax.ShapeDtypeStruct(flat, jnp.bfloat16)),
+        out_shape=(
+            jax.ShapeDtypeStruct(message, jnp.bfloat16),
+            jax.ShapeDtypeStruct((members, devices, SUB, LANES), jnp.bfloat16),
+        ),
         in_specs=[hbm] * 8,
         out_specs=(hbm, hbm),
         scratch_shapes=[pltpu.VMEM(table.shape, table.dtype) for table in constants]
@@ -360,7 +364,7 @@
             [(2, *flat), flat, flat, out_proj.shape]
             + [message] * 3
             + [(devices, SUB, LANES), message]
-            + [message, (devices, SUB, LANES), message, (members, devices, SUB, LANES), flat],
+            + [message, (devices, SUB, LANES), message, (devices, SUB, LANES)],
             jnp.bfloat16,
         )
         + buffers([(2 * rows, 3 * LANES)], jnp.float32)
@@ -381,11 +385,11 @@
         out_shape=(jax.ShapeDtypeStruct(flat, jnp.bfloat16), jax.ShapeDtypeStruct(flat, jnp.float32)),
         in_specs=[hbm] * 2,
         out_specs=(hbm, hbm),
-        scratch_shapes=buffers([message, flat], jnp.bfloat16)
-        + buffers([(width * SUB, LANES)], jnp.float32)
+        scratch_shapes=buffers([message, (members, devices, SUB, LANES)], jnp.bfloat16)
+        + buffers([(width * SUB, LANES)] * 2, jnp.float32)
         + buffers([flat], jnp.bfloat16)
         + buffers([flat], jnp.float32)
-        + [pltpu.SemaphoreType.DMA((4,))],
+        + [pltpu.SemaphoreType.DMA((2,)), pltpu.SemaphoreType.DMA((2 * PARTS,))],
         compiler_params=pltpu.CompilerParams(vmem_limit_bytes=VMEM_LIMIT),
         name="finish",
     )(input_raw, filter_raw)

time: 54.1 us -> 53.4 us (0.987)
  Pallas kernels: 53.3 us -> 52.6 us
    pallas_call x1, Pallas kernels: 51.3 us -> 50.6 us  [per_device(): pl.pallas_call(functools.partial(kernel, members, devices), out_shape=(ja...]
where the time goes in v6:
time: 53.4 us; the launch traced here: 53.3 us
  Pallas kernels  52.6 us (99%)
  between operations  0.64 us (1%)
    pallas_call x1, Pallas kernels, per_device(): pl.pallas_call(functools.partial(kernel, members, devices), out_shape=(ja...  50.6 us
    pallas_call x1, Pallas kernels, per_device(): pl.pallas_call(finish_kernel, out_shape=(jax.ShapeDtypeStruct(flat, jnp.b...  2.06 us

profile of v6, /device:TPU:1, one launch (start us, length us, event | category | flops | bytes accessed | tf_op | source)
XLA Modules:
  0.0 53.3 jit_solution(7234661996419821108)
XLA Ops:
  0.6 50.6 %correlate.1 = (bf16[128,8,128]{2,1,0:T(8,128)(2,1)}, bf16[2,64,8,128]{3,2,1,0:T(8,128)(2,1)}) custom-call(bf16[1024,128]{1,0:T(8,128)(2,1)} %bitcast.3, bf16[1024,128]{1,0:T(8,128)(2,1)} %bitcast.4, bf16[1024,128]{1,0:T(8,128)(2,1)} %taps_hbm.1, bf16[128,256]{1,0:T(8,128)(2,1)} %proj_hbm.1, bf16[1024,1024]{1,0:T(8,128)(2,1)} %constant.8.clone.forward_hbm, ...), custom_call_target="tpu_custom_call" | custom-call | tf_op jit(solution)/shard_map/correlate/pallas_call | solution.py:353
  51.2 2.1 %finish.1 = (bf16[1024,128]{1,0:T(8,128)(2,1)}, f32[1024,128]{1,0:T(8,128)}) custom-call(bf16[128,8,128]{2,1,0:T(8,128)(2,1)} %get-tuple-element.6.input_hbm, bf16[2,64,8,128]{3,2,1,0:T(8,128)(2,1)} %get-tuple-element.7.filter_hbm), custom_call_target="tpu_custom_call" | custom-call | tf_op jit(solution)/shard_map/finish/pallas_call | solution.py:383

commit v7 on v6

--- a/solution.py
+++ b/solution.py
@@ -74,7 +74,7 @@
     forward, inverse, lane, twist, work, cots, signal_ref, taps_ref, proj_ref,
     signal_send, taps_send, grad_send, filter_send, input_send,
     signal_got, taps_got, grad_got, filter_got,
-    outer, pieces, untwisted, spectra, send_sem, recv_sem, load_sem,
+    outer, inner, pieces, untwisted, spectra, send_sem, recv_sem, load_sem,
 ):
     member = lax.axis_index("rep")
     place = lax.axis_index("seq")
@@ -218,10 +218,11 @@
         high, low = pieces[2 * slot], pieces[2 * slot + 1]
         return dot(jnp.concatenate([high, low, high], axis=1), lane[table])
 
-    def transform(values, first):
-        count = values.shape[1] // LANES
-        outer[:, : count * LANES] = dot(forward[...], jnp.concatenate([values, values], axis=0))
-        for at in range(count):
+    def rows_forward(values):
+        outer[:, : values.shape[1]] = dot(forward[...], jnp.concatenate([values, values], axis=0))
+
+    def lanes_forward(first, which):
+        for at in which:
             lanes = slice(at * LANES, (at + 1) * LANES)
             slot = at % 2
             for upper_rows, lower_rows in zip(steps, lower):
@@ -232,16 +233,18 @@
             spectra[first + at] = lane_dot(slot, 0)
 
     def member_rows(ref, at):
-        return ref[at * devices : (at + 1) * devices].reshape(rows, LANES)
+        return ref[pl.ds(at * devices, devices)].reshape(rows, LANES)
 
     def gathered(ref):
-        return jnp.concatenate([member_rows(ref, at) for at in range(members)], axis=1)
+        return jnp.concatenate([member_rows(ref, at) for at in (member, other_member)], axis=1)
 
     arrived(TAP, taps_got)
     arrived(SIG, signal_got)
-    transform(jnp.concatenate([gathered(signal_got), taps_got[...].reshape(rows, LANES)], axis=1), 0)
+    rows_forward(jnp.concatenate([gathered(signal_got), taps_got[...].reshape(rows, LANES)], axis=1))
+    lanes_forward(0, (0, 1, 2))
     arrived(GRAD, grad_got)
-    transform(gathered(grad_got), 3)
+    rows_forward(gathered(grad_got))
+    lanes_forward(3, (0,))
 
     def conj_product(pairs, at_rows):
         real_total = imag_total = None
@@ -260,9 +263,9 @@
             pieces[2 * slot, upper_rows, real_lanes] = real.astype(jnp.bfloat16)
             pieces[2 * slot, upper_rows, imag_lanes] = imag.astype(jnp.bfloat16)
         high = pieces[2 * slot]
-        outer[:rows, : 2 * LANES] = dot(jnp.concatenate([high, high], axis=1), lane[1, 2 * LANES :])
+        inner[...] = dot(jnp.concatenate([high, high], axis=1), lane[1, 2 * LANES :])
         for upper_rows, lower_rows in zip(steps, lower):
-            real, imag = outer[upper_rows, real_lanes], outer[upper_rows, imag_lanes]
+            real, imag = inner[upper_rows, real_lanes], inner[upper_rows, imag_lanes]
             cosine, sine = twist[0, upper_rows], twist[1, upper_rows]
             untwisted[upper_rows, lanes] = (real * cosine - imag * sine).astype(jnp.bfloat16)
             untwisted[lower_rows, lanes] = (imag * cosine + real * sine).astype(jnp.bfloat16)
@@ -271,6 +274,19 @@
         values = untwisted[:, lanes]
         return dot(inverse[...], jnp.concatenate([values, values], axis=0)).astype(jnp.bfloat16)
 
+    def input_result(turn):
+        at = other_member if turn else member
+        lanes = slice((1 + turn) * LANES, (2 + turn) * LANES)
+        untransform(((3 + turn, 2),), 1, lanes)
+        input_send[pl.ds(at * devices, devices)] = rows_inverse(lanes).reshape(devices, SUB, LANES)
+
+        def send_input(at_place):
+            remote(INP, input_send.at[at * devices + at_place], input_got.at[me], device(at, at_place, half)).start()
+
+        around(place, devices, 0 if turn else 1, send_input)
+
+    input_result(0)
+    lanes_forward(3, (1,))
     untransform(((3, 0), (4, 1)), 0, slice(0, LANES))
     filter_send[...] = rows_inverse(slice(0, LANES)).reshape(devices, SUB, LANES)
     others_of_member(
@@ -279,17 +295,7 @@
         ).start()
     )
     pltpu.make_async_copy(filter_send.at[place], filter_got.at[place], recv_sem.at[FILT]).start()
-
-    for turn in range(members):
-        at = other_member if turn else member
-        lanes = slice((1 + turn) * LANES, (2 + turn) * LANES)
-        untransform(((3 + at, 2),), 1 - turn, lanes)
-        input_send[pl.ds(at * devices, devices)] = rows_inverse(lanes).reshape(devices, SUB, LANES)
-
-        def send_input(at_place, at=at):
-            remote(INP, input_send.at[at * devices + at_place], input_got.at[me], device(at, at_place, half)).start()
-
-        around(place, devices, 0 if turn else 1, send_input)
+    input_result(1)
     pltpu.make_async_copy(input_send.at[me], input_got.at[me], recv_sem.at[INP]).start()
 
     arrived(FILT, filter_got)
@@ -367,7 +373,7 @@
             + [message, (devices, SUB, LANES), message, (devices, SUB, LANES)],
             jnp.bfloat16,
         )
-        + buffers([(2 * rows, 3 * LANES)], jnp.float32)
+        + buffers([(2 * rows, 3 * LANES), (rows, 2 * LANES)], jnp.float32)
         + buffers([(4, rows, 2 * LANES), (2 * rows, 3 * LANES)], jnp.bfloat16)
         + buffers([(5, rows, 2 * LANES)], jnp.float32)
         + [

time: 53.4 us -> 54.6 us (1.022)
  Pallas kernels: 52.6 us -> 53.9 us
    pallas_call x1, Pallas kernels: 50.6 us -> 51.8 us  [per_device(): pl.pallas_call(functools.partial(kernel, members, devices), out_shape=(ja...]
where the time goes in v7:
time: 54.6 us; the launch traced here: 54.5 us
  Pallas kernels  53.9 us (99%)
  between operations  0.64 us (1%)
    pallas_call x1, Pallas kernels, per_device(): pl.pallas_call(functools.partial(kernel, members, devices), out_shape=(ja...  51.8 us
    pallas_call x1, Pallas kernels, per_device(): pl.pallas_call(finish_kernel, out_shape=(jax.ShapeDtypeStruct(flat, jnp.b...  2.06 us

profile of v7, /device:TPU:1, one launch (start us, length us, event | category | flops | bytes accessed | tf_op | source)
XLA Modules:
  0.0 54.5 jit_solution(16085107280171176110)
XLA Ops:
  0.6 51.8 %correlate.1 = (bf16[128,8,128]{2,1,0:T(8,128)(2,1)}, bf16[2,64,8,128]{3,2,1,0:T(8,128)(2,1)}) custom-call(bf16[1024,128]{1,0:T(8,128)(2,1)} %bitcast.3, bf16[1024,128]{1,0:T(8,128)(2,1)} %bitcast.4, bf16[1024,128]{1,0:T(8,128)(2,1)} %taps_hbm.1, bf16[128,256]{1,0:T(8,128)(2,1)} %proj_hbm.1, bf16[1024,1024]{1,0:T(8,128)(2,1)} %constant.8.clone.forward_hbm, ...), custom_call_target="tpu_custom_call" | custom-call | tf_op jit(solution)/shard_map/correlate/pallas_call | solution.py:359
  52.5 2.1 %finish.1 = (bf16[1024,128]{1,0:T(8,128)(2,1)}, f32[1024,128]{1,0:T(8,128)}) custom-call(bf16[128,8,128]{2,1,0:T(8,128)(2,1)} %get-tuple-element.6.input_hbm, bf16[2,64,8,128]{3,2,1,0:T(8,128)(2,1)} %get-tuple-element.7.filter_hbm), custom_call_target="tpu_custom_call" | custom-call | tf_op jit(solution)/shard_map/finish/pallas_call | solution.py:389

commit v8 on v6

--- a/solution.py
+++ b/solution.py
@@ -281,7 +281,7 @@
     pltpu.make_async_copy(filter_send.at[place], filter_got.at[place], recv_sem.at[FILT]).start()
 
     for turn in range(members):
-        at = other_member if turn else member
+        at = member if turn else other_member
         lanes = slice((1 + turn) * LANES, (2 + turn) * LANES)
         untransform(((3 + at, 2),), 1 - turn, lanes)
         input_send[pl.ds(at * devices, devices)] = rows_inverse(lanes).reshape(devices, SUB, LANES)
@@ -289,7 +289,7 @@
         def send_input(at_place, at=at):
             remote(INP, input_send.at[at * devices + at_place], input_got.at[me], device(at, at_place, half)).start()
 
-        around(place, devices, 0 if turn else 1, send_input)
+        around(place, devices, 1 if turn else 0, send_input)
     pltpu.make_async_copy(input_send.at[me], input_got.at[me], recv_sem.at[INP]).start()
 
     arrived(FILT, filter_got)

time: 53.4 us -> 51.6 us (0.966)
  Pallas kernels: 52.6 us -> 50.8 us
    pallas_call x1, Pallas kernels: 50.6 us -> 48.8 us  [per_device(): pl.pallas_call(functools.partial(kernel, members, devices), out_shape=(ja...]
where the time goes in v8:
time: 51.6 us; the launch traced here: 51.5 us
  Pallas kernels  50.8 us (98%)
  between operations  0.64 us (1%)
    pallas_call x1, Pallas kernels, per_device(): pl.pallas_call(functools.partial(kernel, members, devices), out_shape=(ja...  48.8 us
    pallas_call x1, Pallas kernels, per_device(): pl.pallas_call(finish_kernel, out_shape=(jax.ShapeDtypeStruct(flat, jnp.b...  2.06 us

profile of v8, /device:TPU:1, one launch (start us, length us, event | category | flops | bytes accessed | tf_op | source)
XLA Modules:
  0.0 51.5 jit_solution(16524331988017402220)
XLA Ops:
  0.6 48.8 %correlate.1 = (bf16[128,8,128]{2,1,0:T(8,128)(2,1)}, bf16[2,64,8,128]{3,2,1,0:T(8,128)(2,1)}) custom-call(bf16[1024,128]{1,0:T(8,128)(2,1)} %bitcast.3, bf16[1024,128]{1,0:T(8,128)(2,1)} %bitcast.4, bf16[1024,128]{1,0:T(8,128)(2,1)} %taps_hbm.1, bf16[128,256]{1,0:T(8,128)(2,1)} %proj_hbm.1, bf16[1024,1024]{1,0:T(8,128)(2,1)} %constant.8.clone.forward_hbm, ...), custom_call_target="tpu_custom_call" | custom-call | tf_op jit(solution)/shard_map/correlate/pallas_call | solution.py:353
  49.4 2.1 %finish.1 = (bf16[1024,128]{1,0:T(8,128)(2,1)}, f32[1024,128]{1,0:T(8,128)}) custom-call(bf16[128,8,128]{2,1,0:T(8,128)(2,1)} %get-tuple-element.6.input_hbm, bf16[2,64,8,128]{3,2,1,0:T(8,128)(2,1)} %get-tuple-element.7.filter_hbm), custom_call_target="tpu_custom_call" | custom-call | tf_op jit(solution)/shard_map/finish/pallas_call | solution.py:383
